TPU v7x, 256 devices: a whole 4x4x8 slice. The times are simulated.
256 devices in a mesh: ctx: 128 (over x, z, y), head: 2 (over core).
Axes of the slice: x: 4, y: 4, z: 8, core: 2. Of those that a mesh axis runs over, the one named last changes fastest.
Arguments:
- queries: bfloat16 [65536, 2048], P('ctx', 'head'), may hold values from -24 to 24
- keys: bfloat16 [65536, 2048], P('ctx', 'head'), may hold values from -24 to 24
- values: bfloat16 [65536, 2048], P('ctx', 'head'), may hold values from -6 to 6
- prefix_keys: bfloat16 [65536, 2048], P('ctx', 'head'), may hold values from -6 to 6
- prefix_values: bfloat16 [65536, 2048], P('ctx', 'head'), may hold values from -6 to 6
- selected: int32 [2, 512, 8, 3], P('head', 'ctx'), may hold values from 0 to 127, all different within a row; in each aligned block of 32 rows (0 to 31, 32 to 63, ..., all dimensions but the last counted through in order) no two rows name the same one
- out_weight: bfloat16 [2, 1024, 4096], P('head', 'ctx'), may hold values from -0.125 to 0.125
Outputs:
- mixed: bfloat16 [65536, 4096], P('ctx', 'head')
Inputs may be any that keep to these rules, and one draw needn't show every extreme that they name: `selected`: for every head group, tile and head, 3 different prefix blocks. Among the 32 rows of one device (one head group, that device's tiles), no block is named more than 1 times.
All inputs are finite; a program needn't handle non-finite values.
Results may differ from a plain program's by a relative error of at most 0.0056.
Values may be sent and summed in bfloat16 or wider, within the bound.
A program may use at most 128 MiB of HBM per device.

v0:
```python
import jax
import jax.numpy as jnp
from jax import lax
from jax.sharding import PartitionSpec as P

D_HEAD = 128
TILE = 128
BLOCK = 512
TOPK = 3


def in_blocks(shard, dim, length):
    before, after = (shard.shape[:dim], shard.shape[dim + 1 :])
    return jnp.moveaxis(shard.reshape(*before, length, -1, *after), dim, 0)


def summed_on_arrival(shard, axis, dim):
    length = lax.axis_size(axis)
    pieces = lax.all_to_all(in_blocks(shard, dim, length), axis, 0, 0, tiled=True)
    return jnp.sum(pieces, axis=0)


def own_attention(queries, keys, values, head_count):
    tok_rows = queries.shape[0]
    blocks_here = tok_rows // BLOCK
    per_block = BLOCK // TILE
    tile_count = blocks_here * per_block
    shaped_query = queries.reshape(blocks_here, BLOCK, head_count, D_HEAD)
    shaped_key = keys.reshape(blocks_here, BLOCK, head_count, D_HEAD)
    shaped_value = values.reshape(blocks_here, BLOCK, head_count, D_HEAD)
    scores = jnp.einsum(
        "bqhd,bkhd->bhqk", shaped_query, shaped_key, preferred_element_type=jnp.float32
    ) * D_HEAD ** (-0.5)
    visible = jnp.arange(BLOCK)[None, :] <= jnp.arange(BLOCK)[:, None]
    scores = jnp.where(visible, scores, -jnp.inf)
    row_max = jnp.max(scores, axis=3)
    weights = jnp.exp(scores - row_max[..., None])
    row_sum = jnp.sum(weights, axis=3)
    partial_out = jnp.einsum(
        "bhqk,bkhd->bhqd",
        weights.astype(jnp.bfloat16),
        shaped_value,
        preferred_element_type=jnp.float32,
    )
    partial_out = partial_out.reshape(blocks_here, head_count, per_block, TILE, D_HEAD).transpose(
        0, 2, 1, 3, 4
    )
    partial_out = partial_out.reshape(tile_count, head_count, TILE, D_HEAD)
    row_max = (
        row_max.reshape(blocks_here, head_count, per_block, TILE)
        .transpose(0, 2, 1, 3)
        .reshape(tile_count, head_count, TILE)
    )
    row_sum = (
        row_sum.reshape(blocks_here, head_count, per_block, TILE)
        .transpose(0, 2, 1, 3)
        .reshape(tile_count, head_count, TILE)
    )
    return (partial_out, row_max, row_sum)


def attend_slot(query_tile, pair_index, key_table, value_table):
    key_block = key_table[pair_index]
    value_block = value_table[pair_index]
    scores = jnp.einsum(
        "qd,kd->qk", query_tile, key_block, preferred_element_type=jnp.float32
    ) * D_HEAD ** (-0.5)
    row_max = jnp.max(scores, axis=1)
    weights = jnp.exp(scores - row_max[:, None])
    row_sum = jnp.sum(weights, axis=1)
    partial_out = jnp.dot(
        weights.astype(jnp.bfloat16), value_block, preferred_element_type=jnp.float32
    )
    return (partial_out, row_max, row_sum)


def serve_slots(query_slots, pair_slots, key_table, value_table):
    leading = pair_slots.shape
    flat_query = query_slots.reshape((-1,) + query_slots.shape[-2:])
    flat_pairs = pair_slots.reshape(-1)

    def attend_item(slot_item):
        return attend_slot(slot_item[0], slot_item[1], key_table, value_table)

    results = lax.map(attend_item, (flat_query, flat_pairs), batch_size=16)
    return tuple((result_part.reshape(leading + result_part.shape[1:]) for result_part in results))


def shards(queries, keys, values, prefix_keys, prefix_values, selected, out_weight):
    tok_rows, width_local = queries.shape
    head_count = width_local // D_HEAD
    tile_count = tok_rows // TILE
    blocks_here = tok_rows // BLOCK
    peer_count = lax.axis_size("ctx")
    block_total = peer_count * blocks_here
    request_count = tile_count * head_count * TOPK
    capacity = (request_count + block_total - 1) // block_total
    slot_count = capacity * blocks_here
    slot_total = peer_count * slot_count
    picked_ids = selected.reshape(request_count)
    owners = picked_ids // blocks_here
    local_block = picked_ids % blocks_here
    owner_onehot = (owners[:, None] == jnp.arange(peer_count, dtype=jnp.int32)[None, :]).astype(
        jnp.int32
    )
    ranking = jnp.sum((jnp.cumsum(owner_onehot, axis=0) - owner_onehot) * owner_onehot, axis=1)
    slot_of = owners * slot_count + ranking
    request_ids = jnp.arange(request_count, dtype=jnp.int32)
    matches = slot_of[None, :] == jnp.arange(slot_total, dtype=jnp.int32)[:, None]
    filled = jnp.any(matches, axis=1)
    source_of = jnp.sum(jnp.where(matches, request_ids[None, :], 0), axis=1)
    pair_of = local_block * head_count + request_ids // TOPK % head_count
    pair_slots = jnp.sum(jnp.where(matches, pair_of[None, :], 0), axis=1).reshape(
        peer_count, slot_count
    )
    tile_queries = queries.reshape(tile_count, TILE, head_count, D_HEAD).transpose(0, 2, 1, 3)
    tile_queries = tile_queries.reshape(tile_count * head_count, TILE, D_HEAD)
    outgoing = jnp.take(tile_queries, source_of // TOPK, axis=0)
    outgoing = jnp.where(filled[:, None, None], outgoing, jnp.zeros_like(outgoing))
    outgoing = outgoing.reshape(peer_count, slot_count, TILE, D_HEAD)
    key_table = prefix_keys.reshape(blocks_here, BLOCK, head_count, D_HEAD).transpose(0, 2, 1, 3)
    key_table = key_table.reshape(blocks_here * head_count, BLOCK, D_HEAD)
    value_table = prefix_values.reshape(blocks_here, BLOCK, head_count, D_HEAD).transpose(
        0, 2, 1, 3
    )
    value_table = value_table.reshape(blocks_here * head_count, BLOCK, D_HEAD)
    arrived = (
        lax.all_to_all(outgoing, "ctx", split_axis=0, concat_axis=0, tiled=True),
        lax.all_to_all(pair_slots, "ctx", split_axis=0, concat_axis=0, tiled=True),
    )
    answers = serve_slots(arrived[0], arrived[1], key_table, value_table)
    back_out, back_max, back_sum = (
        lax.all_to_all(answers[0], "ctx", split_axis=0, concat_axis=0, tiled=True),
        lax.all_to_all(answers[1], "ctx", split_axis=0, concat_axis=0, tiled=True),
        lax.all_to_all(answers[2], "ctx", split_axis=0, concat_axis=0, tiled=True),
    )
    own_parts = own_attention(queries, keys, values, head_count)
    own_out, own_max, own_sum = own_parts
    sel_out = jnp.take(back_out.reshape(slot_total, TILE, D_HEAD), slot_of, axis=0)
    sel_out = sel_out.reshape(tile_count, head_count, TOPK, TILE, D_HEAD)
    sel_max = jnp.take(back_max.reshape(slot_total, TILE), slot_of, axis=0).reshape(
        tile_count, head_count, TOPK, TILE
    )
    sel_sum = jnp.take(back_sum.reshape(slot_total, TILE), slot_of, axis=0).reshape(
        tile_count, head_count, TOPK, TILE
    )
    highest = jnp.maximum(own_max, jnp.max(sel_max, axis=2))
    own_factor = jnp.exp(own_max - highest)
    sel_factor = jnp.exp(sel_max - highest[:, :, None, :])
    numerator = own_factor[..., None] * own_out + jnp.sum(sel_factor[..., None] * sel_out, axis=2)
    denominator = own_factor * own_sum + jnp.sum(sel_factor * sel_sum, axis=2)
    attention = (
        (numerator / denominator[..., None]).transpose(0, 2, 1, 3).reshape(tok_rows, width_local)
    )
    attention = attention.astype(jnp.bfloat16)
    mixed_part = jnp.dot(
        attention,
        lax.all_gather(out_weight, "ctx", axis=1, tiled=True)[0],
        preferred_element_type=jnp.float32,
    )
    return summed_on_arrival(mixed_part, "head", 1).astype(jnp.bfloat16)


def solution(mesh):
    return jax.shard_map(
        shards,
        mesh=mesh,
        in_specs=(
            P("ctx", "head"),
            P("ctx", "head"),
            P("ctx", "head"),
            P("ctx", "head"),
            P("ctx", "head"),
            P("head", "ctx", None, None),
            P("head", "ctx", None),
        ),
        out_specs=P("ctx", "head"),
        check_vma=False,
    )
```

profile of v0, /device:TPU:1, one launch (start us, length us, event | category | flops | bytes accessed | tf_op | source)
XLA Modules:
  0.0 564.5 jit_solution(2384505471579033138)
XLA Ops:
  8.8 16.3 %all-to-all-start.1 = ((s32[128,1,1]{2,1,0:T(1,128)}), s32[128,1,1]{2,1,0:T(1,128)S(1)}, u32[]{:S(2)}, u32[]{:S(2)}) async-start(s32[128,1,1]{2,1,0:T(1,128)} %copy.99), calls=%async_computation.1 | async-start | bytes 131072 | tf_op jit(solution)/shard_map/all_to_all | solution.py:129
  30.2 4.0 fusion.24
  35.7 12.5 %all-to-all-start = ((bf16[128,1,128,128]{3,2,1,0:T(8,128)(2,1)}), bf16[128,1,128,128]{3,2,1,0:T(8,128)(2,1)}, u32[]{:S(2)}, u32[]{:S(2)}) async-start(bf16[128,1,128,128]{3,2,1,0:T(8,128)(2,1)} %fusion.24), calls=%async_computation | async-start | bytes 8388608 | tf_op jit(solution)/shard_map/all_to_all | solution.py:128
  53.3 87.4 %all-to-all-done = bf16[128,1,128,128]{3,2,1,0:T(8,128)(2,1)} async-done(((bf16[128,1,128,128]{3,2,1,0:T(8,128)(2,1)}), bf16[128,1,128,128]{3,2,1,0:T(8,128)(2,1)}, u32[]{:S(2)}, u32[]{:S(2)}) %all-to-all-start) | async-done | bytes 4194336 | tf_op jit(solution)/shard_map/all_to_all | solution.py:128
  140.6 109.5 %while.14 = (s32[]{:T(128)}, f32[8,16,128,128]{3,2,1,0:T(8,128)}, f32[8,16,128]{2,1,0:T(8,128)}, f32[8,16,128]{2,1,0:T(8,128)S(1)}, bf16[8,16,128,128]{3,2,1,0:T...) while((s32[]{:T(128)}, f32[8,16,128,128]{3,2,1,0:T(8,128)}, ...), condition=%wide.region_9.10_spmd, body=%wide.region_6.9_spmd.sunk | while | flops 545255552 | bytes 43583612 | solution.py:85
  150.2 4.1 fusion.67
  163.8 4.2 fusion.67
  177.6 4.1 fusion.67
  191.2 4.1 fusion.67
  204.9 4.1 fusion.67
  218.6 4.2 fusion.67
  232.3 4.2 fusion.67
  246.0 4.1 fusion.67
  250.1 21.3 %all_to_all.34 = f32[128,1,128]{2,1,0:T(1,128)S(1)} all-to-all(f32[128,1,128]{2,1,0:T(1,128)S(1)} %bitcast.181), channel_id=1, replica_groups=mesh['ctx'=128,'head'=2] {'ctx'}, dimensions={0} | all-to-all | bytes 131072 | tf_op jit(solution)/shard_map/all_to_all | solution.py:135
  271.4 6.1 %all-to-all-start.2 = ((f32[128,1,128]{2,1,0:T(1,128)}), f32[128,1,128]{2,1,0:T(1,128)S(1)}, u32[]{:S(2)}, u32[]{:S(2)}) async-start(f32[128,1,128]{2,1,0:T(1,128)} %bitcast.23), calls=%async_computation.2 | async-start | bytes 131072 | tf_op jit(solution)/shard_map/all_to_all | solution.py:134
  278.2 9.8 %all-to-all-done.2 = f32[128,1,128]{2,1,0:T(1,128)S(1)} async-done(((f32[128,1,128]{2,1,0:T(1,128)}), f32[128,1,128]{2,1,0:T(1,128)S(1)}, u32[]{:S(2)}, u32[]{:S(2)}) %all-to-all-start.2) | async-done | bytes 65568 | tf_op jit(solution)/shard_map/all_to_all | solution.py:134
  288.0 7.6 %all-to-all-start.3 = ((f32[128,1,128,128]{3,2,1,0:T(8,128)}), f32[128,1,128,128]{3,2,1,0:T(8,128)}, u32[]{:S(2)}, u32[]{:S(2)}) async-start(f32[128,1,128,128]{3,2,1,0:T(8,128)} %bitcast.173), calls=%async_computation.3 | async-start | bytes 16777216 | tf_op jit(solution)/shard_map/all_to_all | solution.py:133
  303.6 203.0 %all-gather.2.cloned.1.call-done = bf16[1,1024,4096]{2,1,0:T(8,128)(2,1)} async-done(((bf16[1,8,4096]{2,1,0:T(8,128)(2,1)}), bf16[1,1024,4096]{2,1,0:T(8,128)(2,1)}) %all-gather.2.cloned.1.call-update) | async-done | bytes 8388624 | tf_op jit(solution)/shard_map/all_gather | solution.py:158
  506.5 11.9 %copy.109 = bf16[4096,1024]{1,0:T(8,128)(2,1)} copy(bf16[4096,1024]{0,1:T(8,128)(2,1)} %bitcast.171) | data formatting | bytes 16777216 | tf_op jit(solution)/shard_map/dot_general | solution.py:156
  518.5 7.0 %gather_fusion.3 = f32[96,128,128]{2,1,0:T(8,128)} fusion(f32[128,128,128]{2,1,0:T(8,128)} %bitcast.30, s32[1024]{0:T(1024)S(1)} %pad_clamp_fusion), kind=kCustom, calls=%fused_computation.5 | custom fusion | bytes 12583296 | tf_op jit(solution)/shard_map/jit(_take)/gather | solution.py:139
  525.4 4.6 multiply_reduce_fusion.1
  532.5 7.0 %convolution_bitcast_fusion = f32[2,512,2048]{2,1,0:T(8,128)S(1)} fusion(bf16[512,1024,1]{1,0,2:T(8,128)(2,1)S(1)} %reshape.379, bf16[2,2048,1024]{2,1,0:T(8,128)(2,1)} %bitcast.172), kind=kOutput, calls=%fused_computation.32 | convolution fusion | flops 4294967296 | bytes 17825792 | tf_op jit(solution)/shard_map/dot_general | solution.py:156
  539.5 12.0 %all_to_all.35 = f32[2,512,2048]{2,1,0:T(8,128)} all-to-all(f32[2,512,2048]{2,1,0:T(8,128)S(1)} %convolution_bitcast_fusion), channel_id=1, replica_groups=mesh['ctx'=128,'head'=2] {'head'}, dimensions={0} | all-to-all | bytes 16777216 | tf_op jit(solution)/shard_map/all_to_all | solution.py:19
  551.5 6.1 %reduce_sum.87 = bf16[512,2048]{1,0:T(8,128)(2,1)} reduce(f32[2,512,2048]{2,1,0:T(8,128)} %all_to_all.35, f32[]{:T(128)} %constant.121.clone.1), dimensions={0}, to_apply=%region_14.16 | reduce | flops 1048576 | bytes 10485764 | tf_op jit(solution)/shard_map/reduce_sum | solution.py:20
  (132 shorter events, 100.7 us)
Async XLA Ops:
  6.5 289.7 %copy-start = (bf16[512,1024]{1,0:T(8,128)(2,1)S(1)}, bf16[512,1024]{1,0:T(8,128)(2,1)}, u32[]{:S(2)}) copy-start(bf16[512,1024]{1,0:T(8,128)(2,1)} %param.12) | copy-start | bytes 3145732
  8.8 26.8 %all-to-all-start.1 = ((s32[128,1,1]{2,1,0:T(1,128)}), s32[128,1,1]{2,1,0:T(1,128)S(1)}, u32[]{:S(2)}, u32[]{:S(2)}) async-start(s32[128,1,1]{2,1,0:T(1,128)} %copy.99), calls=%async_computation.1 | async-start | bytes 131072 | tf_op jit(solution)/shard_map/all_to_all | solution.py:129
  34.2 14.0 %copy-start.3 = (bf16[512,1024]{1,0:T(8,128)(2,1)S(1)}, bf16[512,1024]{1,0:T(8,128)(2,1)}, u32[]{:S(2)}) copy-start(bf16[512,1024]{1,0:T(8,128)(2,1)} %param.14) | copy-start | bytes 3145732
  34.2 15.3 %copy-start.4 = (bf16[512,1024]{1,0:T(8,128)(2,1)S(1)}, bf16[512,1024]{1,0:T(8,128)(2,1)}, u32[]{:S(2)}) copy-start(bf16[512,1024]{1,0:T(8,128)(2,1)} %param.15) | copy-start | bytes 3145732
  35.7 105.0 %all-to-all-start = ((bf16[128,1,128,128]{3,2,1,0:T(8,128)(2,1)}), bf16[128,1,128,128]{3,2,1,0:T(8,128)(2,1)}, u32[]{:S(2)}, u32[]{:S(2)}) async-start(bf16[128,1,128,128]{3,2,1,0:T(8,128)(2,1)} %fusion.24), calls=%async_computation | async-start | bytes 8388608 | tf_op jit(solution)/shard_map/all_to_all | solution.py:128
  144.4 2.0 copy-start.2
  158.1 2.0 copy-start.2
  171.8 2.0 copy-start.2
  185.4 2.0 copy-start.2
  199.1 2.0 copy-start.2
  212.8 2.0 copy-start.2
  226.5 2.0 copy-start.2
  240.2 2.0 copy-start.2
  271.4 16.6 %all-to-all-start.2 = ((f32[128,1,128]{2,1,0:T(1,128)}), f32[128,1,128]{2,1,0:T(1,128)S(1)}, u32[]{:S(2)}, u32[]{:S(2)}) async-start(f32[128,1,128]{2,1,0:T(1,128)} %bitcast.23), calls=%async_computation.2 | async-start | bytes 131072 | tf_op jit(solution)/shard_map/all_to_all | solution.py:134
  277.5 229.0 %all-gather.2.cloned.1.call-start = ((), (), s32[]{:S(2)}) async-start(), calls=%async_computation.6 | async-start | bytes 8454144 | tf_op jit(solution)/shard_map/all_gather | solution.py:158
  288.0 7.9 %copy-start.6 = (s32[1,4,8,3]{2,1,3,0:T(4,128)S(1)}, s32[1,4,8,3]{2,1,3,0:T(4,128)}, u32[]{:S(2)}) copy-start(s32[1,4,8,3]{2,1,3,0:T(4,128)} %param.16) | copy-start | bytes 1156
  288.0 8.2 %copy-start.5 = (bf16[512,1024]{1,0:T(8,128)(2,1)S(1)}, bf16[512,1024]{1,0:T(8,128)(2,1)}, u32[]{:S(2)}) copy-start(bf16[512,1024]{1,0:T(8,128)(2,1)} %param.11) | copy-start | bytes 3145732
  288.0 230.4 %all-to-all-start.3 = ((f32[128,1,128,128]{3,2,1,0:T(8,128)}), f32[128,1,128,128]{3,2,1,0:T(8,128)}, u32[]{:S(2)}, u32[]{:S(2)}) async-start(f32[128,1,128,128]{3,2,1,0:T(8,128)} %bitcast.173), calls=%async_computation.3 | async-start | bytes 16777216 | tf_op jit(solution)/shard_map/all_to_all | solution.py:133
  297.8 1.8 copy-start.7
  539.5 18.1 %copy-start.1 = (bf16[512,1024]{1,0:T(8,128)(2,1)S(1)}, bf16[512,1024]{1,0:T(8,128)(2,1)}, u32[]{:S(2)}) copy-start(bf16[512,1024]{1,0:T(8,128)(2,1)} %param.12) | copy-start | bytes 3145732
Sparse Core Ops, SparseCore 0:
  281.8 224.6 all-gather.1
where the time goes:
time: 569 us; the launch traced here: 564 us
  waiting for transfers between devices  302 us (53%)
  local copies, waits for them, and re-layouts  82.1 us (14%)
  matrix products  58.7 us (10%)
  starting transfers between devices  42.6 us (7%)
  blocking collectives  33.3 us (6%)
  other arithmetic  31.6 us (6%)
  between operations  13.7 us (2%)
    all_gather x1, waiting for transfers between devices, shards(): lax.all_gather(out_weight, 'ctx', axis=1, tiled=True)[0]  203 us
    all_to_all x1, waiting for transfers between devices, shards(): lax.all_to_all(outgoing, 'ctx', split_axis=0, concat_axis=0, tiled=True)  87.4 us
    dot_general x8, matrix products, attend_slot(): jnp.dot(weights.astype(jnp.bfloat16), value_block, preferred_element_type...  33.2 us
    all_to_all x1, blocking collectives, shards(): lax.all_to_all(answers[2], 'ctx', split_axis=0, concat_axis=0, tiled=True)  21.3 us
    all_to_all x1, starting transfers between devices, shards(): lax.all_to_all(pair_slots, 'ctx', split_axis=0, concat_axis=0, tiled=True)  16.3 us
    while x16, local copies, waits for them, and re-layouts  15.6 us
    gather x8, local copies, waits for them, and re-layouts, attend_slot(): key_block = key_table[pair_index]  15.3 us
    gather x8, local copies, waits for them, and re-layouts, attend_slot(): value_block = value_table[pair_index]  15.3 us
  transfers between devices with their start and end apart: 5, of which 4 were waited for; matrix products, arithmetic and copies ran while one was open for 6% of the time, Pallas kernels for 0%

commit v1 on v0

v1 whole, which is shorter than its diff:
```python
import functools
import math

import jax
import jax.numpy as jnp
from jax import lax
from jax.experimental import pallas as pl
from jax.experimental.pallas import tpu as pltpu
from jax.sharding import PartitionSpec as P

D_HEAD = 128
TILE = 128
BLOCK = 512
TOPK = 3
TILES = 4
HEADS = 8
ITEMS = TILES * HEADS
NX, NZ, NY = 4, 8, 4
PEERS = NX * NZ * NY
SCALE2 = D_HEAD**-0.5 * math.log2(math.e)


def coords(index):
    return index // (NZ * NY), (index // NY) % NZ, index % NY


def place(x, z, y):
    return (x * NZ + z) * NY + y


def offset_of(step):
    dz = (step * 3) % NZ
    dy = (step // NZ) % NY
    dx = (step // (NZ * NY)) % NX
    return dx, dz, dy


def moved(me, step, sign):
    x, z, y = coords(me)
    dx, dz, dy = offset_of(step)
    return place((x + sign * dx + NX) % NX, (z + sign * dz + NZ) % NZ, (y + sign * dy + NY) % NY)


def attend(key_block, value_block_t, query, mask=None):
    scores = lax.dot_general(
        key_block, query, (((1,), (1,)), ((), ())), preferred_element_type=jnp.float32
    )
    scores = scores * SCALE2
    if mask is not None:
        scores = jnp.where(mask, scores, -jnp.inf)
    top = jnp.max(scores, axis=0, keepdims=True)
    weights = jnp.exp2(scores - top)
    total = jnp.sum(weights, axis=0, keepdims=True)
    out = lax.dot_general(
        value_block_t,
        weights.astype(jnp.bfloat16),
        (((1,), (0,)), ((), ())),
        preferred_element_type=jnp.float32,
    )
    return out / total, top + jnp.log2(total)


def layer_kernel(
    wanted_ref,
    picked_ref,
    wanted_row_ref,
    q_ref,
    k_ref,
    v_ref,
    pk_ref,
    pv_ref,
    out_ref,
    items,
    send_q,
    recv_q,
    send_o,
    recv_o,
    send_l,
    recv_l,
    vt,
    own_o,
    own_l,
    table,
    table_s,
    table_sem,
    q_send_sem,
    q_recv_sem,
    o_send_sem,
    o_recv_sem,
    l_send_sem,
    l_recv_sem,
    t_send_sem,
    t_recv_sem,
    h_send_sem,
    h_recv_sem,
):
    me = lax.axis_index("ctx")
    core = lax.axis_index("head")
    x, z, y = coords(me)
    sign = 1 - 2 * core

    barrier = pltpu.get_barrier_semaphore()

    def greet(step, carry):
        pl.semaphore_signal(
            barrier,
            inc=1,
            device_id={"ctx": moved(me, step, 1)},
            device_id_type=pl.DeviceIdType.MESH,
        )
        return carry

    lax.fori_loop(1, PEERS, greet, 0)
    pl.semaphore_signal(
        barrier, inc=1, device_id={"head": 1 - core}, device_id_type=pl.DeviceIdType.MESH
    )

    for t in range(TILES):
        for h in range(HEADS):
            items[t * HEADS + h] = q_ref[
                t * TILE : (t + 1) * TILE, h * D_HEAD : (h + 1) * D_HEAD
            ]
    table[me] = wanted_row_ref[...]
    pl.semaphore_wait(barrier, PEERS)

    def table_copy(slot, rows, start, target):
        return pltpu.make_async_remote_copy(
            src_ref=table.at[pl.ds(start, rows)],
            dst_ref=table.at[pl.ds(start, rows)],
            send_sem=t_send_sem.at[slot],
            recv_sem=t_recv_sem.at[slot],
            device_id={"ctx": target},
            device_id_type=pl.DeviceIdType.MESH,
        )

    y_copies = [table_copy(d - 1, 1, me, place(x, z, (y + d) % NY)) for d in range(1, NY)]
    for c in y_copies:
        c.start()

    def q_copy(target, slot):
        return pltpu.make_async_remote_copy(
            src_ref=send_q.at[target],
            dst_ref=recv_q.at[slot],
            send_sem=q_send_sem.at[target],
            recv_sem=q_recv_sem.at[slot],
            device_id={"ctx": target},
            device_id_type=pl.DeviceIdType.MESH,
        )

    def send_query(step, carry):
        target = moved(me, step, sign)
        send_q[target] = items[wanted_ref[target]]
        q_copy(target, me).start()
        return carry

    lax.fori_loop(1, 17, send_query, 0)
    for d in range(1, NY):
        table_copy(d - 1, 1, place(x, z, (y - d + NY) % NY), me).wait_recv()
    z_copies = [
        table_copy(2 + d, NY, place(x, z, 0), place(x, (z + d) % NZ, y)) for d in range(1, NZ)
    ]
    for c in z_copies:
        c.start()
    lax.fori_loop(17, 49, send_query, 0)
    for d in range(1, NZ):
        table_copy(2 + d, NY, place(x, (z - d + NZ) % NZ, 0), me).wait_recv()
    x_copies = [
        table_copy(9 + d, NZ * NY, place(x, 0, 0), place((x + d) % NX, z, y))
        for d in range(1, NX)
    ]
    for c in x_copies:
        c.start()
    lax.fori_loop(49, PEERS, send_query, 0)

    for t in range(TILES):
        depth = (t + 1) * TILE
        row = lax.broadcasted_iota(jnp.int32, (depth, TILE), 0)
        column = lax.broadcasted_iota(jnp.int32, (depth, TILE), 1)
        mask = row <= column + t * TILE
        for h in range(HEADS):
            columns = slice(h * D_HEAD, (h + 1) * D_HEAD)
            out, lse = attend(
                k_ref[:depth, columns],
                v_ref[:depth, columns].T,
                q_ref[t * TILE : (t + 1) * TILE, columns],
                mask,
            )
            own_o[t * HEADS + h] = out
            own_l[t * HEADS + h] = lse
    for h in range(HEADS):
        columns = slice(h * D_HEAD, (h + 1) * D_HEAD)
        vt[h] = pv_ref[:, columns].T

    for d in range(1, NX):
        table_copy(9 + d, NZ * NY, place((x - d + NX) % NX, 0, 0), me).wait_recv()
    to_scalars = pltpu.make_async_copy(table, table_s, table_sem)
    to_scalars.start()
    to_scalars.wait()

    def o_copy(target, slot):
        return pltpu.make_async_remote_copy(
            src_ref=send_o.at[target],
            dst_ref=recv_o.at[slot],
            send_sem=o_send_sem.at[target],
            recv_sem=o_recv_sem.at[slot],
            device_id={"ctx": target},
            device_id_type=pl.DeviceIdType.MESH,
        )

    def l_copy(target, slot):
        return pltpu.make_async_remote_copy(
            src_ref=send_l.at[target],
            dst_ref=recv_l.at[slot],
            send_sem=l_send_sem.at[target],
            recv_sem=l_recv_sem.at[slot],
            device_id={"ctx": target},
            device_id_type=pl.DeviceIdType.MESH,
        )

    def answer(source, query):
        head = table_s[source, 0, me] % HEADS
        return attend(pk_ref[head], vt[head], query)

    out, lse = answer(me, items[wanted_ref[me]])
    recv_o[me] = out.astype(jnp.bfloat16)
    recv_l[me] = lse

    def serve(step, carry):
        source = moved(me, step, -sign)
        q_copy(me, source).wait_recv()
        out, lse = answer(source, recv_q[source])
        send_o[source] = out.astype(jnp.bfloat16)
        send_l[source] = lse
        o_copy(source, me).start()
        l_copy(source, me).start()
        return carry

    lax.fori_loop(1, PEERS, serve, 0)

    def settle(step, carry):
        server = moved(me, step, sign)
        o_copy(me, server).wait_recv()
        l_copy(me, server).wait_recv()
        return carry

    lax.fori_loop(1, PEERS, settle, 0)

    def h_copy(t):
        return pltpu.make_async_remote_copy(
            src_ref=out_ref.at[core, pl.ds(t * TILE, TILE)],
            dst_ref=out_ref.at[core, pl.ds(t * TILE, TILE)],
            send_sem=h_send_sem.at[t],
            recv_sem=h_recv_sem.at[t],
            device_id={"head": 1 - core},
            device_id_type=pl.DeviceIdType.MESH,
        )

    for t in range(TILES):
        for h in range(HEADS):
            item = t * HEADS + h
            slots = [picked_ref[item * TOPK + j] for j in range(TOPK)]
            lses = [own_l[item]] + [recv_l[s] for s in slots]
            highest = functools.reduce(jnp.maximum, lses)
            factors = [jnp.exp2(v - highest) for v in lses]
            total = functools.reduce(jnp.add, factors)
            mixed = factors[0] * own_o[item]
            for f, s in zip(factors[1:], slots):
                mixed = mixed + f * recv_o[s].astype(jnp.float32)
            mixed = mixed / total
            out_ref[core, t * TILE : (t + 1) * TILE, h * D_HEAD : (h + 1) * D_HEAD] = (
                mixed.T.astype(jnp.bfloat16)
            )
        h_copy(t).start()
    for t in range(TILES):
        pltpu.make_async_remote_copy(
            src_ref=out_ref.at[1 - core, pl.ds(t * TILE, TILE)],
            dst_ref=out_ref.at[1 - core, pl.ds(t * TILE, TILE)],
            send_sem=h_send_sem.at[t],
            recv_sem=h_recv_sem.at[t],
            device_id={"head": 1 - core},
            device_id_type=pl.DeviceIdType.MESH,
        ).wait_recv()
    for t in range(TILES):
        h_copy(t).wait_send()

    def drain(step, carry):
        target = moved(me, step, sign)
        q_copy(target, me).wait_send()
        source = moved(me, step, -sign)
        o_copy(source, me).wait_send()
        l_copy(source, me).wait_send()
        return carry

    lax.fori_loop(1, PEERS, drain, 0)
    for c in y_copies + z_copies + x_copies:
        c.wait_send()


def attention_layer(wanted, picked, queries, keys, values, prefix_keys, prefix_values):
    vmem = pl.BlockSpec(memory_space=pltpu.VMEM)
    smem = pl.BlockSpec(memory_space=pltpu.SMEM)
    slots = (PEERS, TILE, D_HEAD)
    sem = pltpu.SemaphoreType.DMA
    return pl.pallas_call(
        layer_kernel,
        out_shape=jax.ShapeDtypeStruct((2, BLOCK, HEADS * D_HEAD), jnp.bfloat16),
        in_specs=[smem, smem, vmem, vmem, vmem, vmem, vmem, vmem],
        out_specs=vmem,
        scratch_shapes=[
            pltpu.VMEM((ITEMS, TILE, D_HEAD), jnp.bfloat16),
            pltpu.VMEM(slots, jnp.bfloat16),
            pltpu.VMEM(slots, jnp.bfloat16),
            pltpu.VMEM(slots, jnp.bfloat16),
            pltpu.VMEM(slots, jnp.bfloat16),
            pltpu.VMEM((PEERS, 1, TILE), jnp.float32),
            pltpu.VMEM((PEERS, 1, TILE), jnp.float32),
            pltpu.VMEM((HEADS, D_HEAD, BLOCK), jnp.bfloat16),
            pltpu.VMEM((ITEMS, D_HEAD, TILE), jnp.float32),
            pltpu.VMEM((ITEMS, 1, TILE), jnp.float32),
            pltpu.VMEM((PEERS, 1, PEERS), jnp.int32),
            pltpu.SMEM((PEERS, 1, PEERS), jnp.int32),
            sem,
            sem((PEERS,)),
            sem((PEERS,)),
            sem((PEERS,)),
            sem((PEERS,)),
            sem((PEERS,)),
            sem((PEERS,)),
            sem((13,)),
            sem((13,)),
            sem((TILES,)),
            sem((TILES,)),
        ],
        compiler_params=pltpu.CompilerParams(
            collective_id=0, has_side_effects=True, vmem_limit_bytes=48 * 1024 * 1024
        ),
        cost_estimate=pl.CostEstimate(
            flops=6_000_000_000, bytes_accessed=700_000_000, transcendentals=10_000_000
        ),
    )(wanted, picked, wanted[None], queries, keys, values, prefix_keys, prefix_values)


def shards(queries, keys, values, prefix_keys, prefix_values, selected, out_weight):
    picked = selected.reshape(ITEMS * TOPK)
    matches = picked[None, :] == jnp.arange(PEERS, dtype=jnp.int32)[:, None]
    item_ids = jnp.arange(ITEMS * TOPK, dtype=jnp.int32) // TOPK
    wanted = jnp.sum(jnp.where(matches, item_ids[None, :], 0), axis=1)
    features = out_weight.shape[2] // 2
    swapped = lax.all_to_all(
        out_weight[0].reshape(-1, 2, features), "head", split_axis=1, concat_axis=1, tiled=True
    )
    weight = lax.all_gather(swapped.transpose(1, 0, 2), "ctx", axis=1, tiled=True)
    head_keys = prefix_keys.reshape(BLOCK, HEADS, D_HEAD).transpose(1, 0, 2)
    attention = attention_layer(
        wanted, picked, queries, keys, values, head_keys, prefix_values
    )
    return jnp.einsum(
        "gtr,grf->tf", attention, weight, preferred_element_type=jnp.float32
    ).astype(jnp.bfloat16)


def solution(mesh):
    return jax.shard_map(
        shards,
        mesh=mesh,
        in_specs=(
            P("ctx", "head"),
            P("ctx", "head"),
            P("ctx", "head"),
            P("ctx", "head"),
            P("ctx", "head"),
            P("head", "ctx", None, None),
            P("head", "ctx", None),
        ),
        out_specs=P("ctx", "head"),
        check_vma=False,
    )
```

time: 569 us -> 291 us (0.51)
  waiting for transfers between devices: 302 us -> 0.04 us
  Pallas kernels: 0 us -> 251 us
  local copies, waits for them, and re-layouts: 82.1 us -> 7.41 us
  matrix products: 58.7 us -> 9.84 us
  starting transfers between devices: 42.6 us -> 0.01 us
  other arithmetic: 31.6 us -> 0.12 us
  blocking collectives: 33.3 us -> 8.33 us
    pallas_call x0 -> x1, Pallas kernels: none -> 251 us  [attention_layer(): pl.pallas_call(layer_kernel, out_shape=jax.ShapeDtypeStruct((2, BLOCK, HE...]
    all_gather x1, waiting for transfers between devices: 203 us -> 0.02 us  [shards(): lax.all_gather(swapped.transpose(1, 0, 2), 'ctx', axis=1, tiled=True)]
    all_to_all x4 -> x0, waiting for transfers between devices: 98.6 us -> none  [the longest x1 87.4 us: shards(): lax.all_to_all(outgoing, 'ctx', split_axis=0, concat_axis=0, tiled=True)]
    dot_general x19 -> x1, matrix products: 58.7 us -> 9.84 us  [shards(): jnp.einsum('gtr,grf->tf', attention, weight, preferred_element_type=jnp.f...]
    all_to_all x4 -> x0, starting transfers between devices: 42.5 us -> none  [the longest x1 16.3 us: shards(): lax.all_to_all(pair_slots, 'ctx', split_axis=0, concat_axis=0, tiled=True)]
    gather x20 -> x0, local copies, waits for them, and re-layouts: 41.8 us -> none  [the longest x8 15.3 us: attend_slot(): key_block = key_table[pair_index]]
    all_to_all x2 -> x1, blocking collectives: 33.3 us -> 8.33 us  [shards(): lax.all_to_all(out_weight[0].reshape(-1, 2, features), 'head', split_axis...]
    reduce_sum x14 -> x1, other arithmetic: 23.2 us -> 0.11 us  [shards(): wanted = jnp.sum(jnp.where(matches, item_ids[None, :], 0), axis=1)]
  transfers between devices with their start and end apart: 5 -> 1, of which waited for: 4 -> 0; matrix products, arithmetic and copies ran while one was open for 6% -> 2% of each run, Pallas kernels for 0% -> 87%
where the time goes in v1:
time: 291 us; the launch traced here: 290 us
  Pallas kernels  251 us (86%)
  between operations  13.5 us (5%)
  matrix products  9.84 us (3%)
  blocking collectives  8.33 us (3%)
  local copies, waits for them, and re-layouts  7.41 us (3%)
    pallas_call x1, Pallas kernels, attention_layer(): pl.pallas_call(layer_kernel, out_shape=jax.ShapeDtypeStruct((2, BLOCK, HE...  251 us
    dot_general x1, matrix products, shards(): jnp.einsum('gtr,grf->tf', attention, weight, preferred_element_type=jnp.f...  9.84 us
    all_to_all x1, blocking collectives, shards(): lax.all_to_all(out_weight[0].reshape(-1, 2, features), 'head', split_axis...  8.33 us
  transfers between devices with their start and end apart: 1, of which 0 were waited for; matrix products, arithmetic and copies ran while one was open for 2% of the time, Pallas kernels for 87%

profile of v1, /device:TPU:1, one launch (start us, length us, event | category | flops | bytes accessed | tf_op | source)
XLA Modules:
  0.0 290.2 jit_solution(18229516026982953797)
XLA Ops:
  6.5 0.0 all-gather.2.cloned.1.call-start
  6.5 8.3 %all_to_all.5 = bf16[8,2,2048]{2,0,1:T(8,128)(2,1)} all-to-all(bf16[8,2,2048]{2,0,1:T(8,128)(2,1)} %bitcast.15), channel_id=1, replica_groups=mesh['ctx'=128,'head'=2] {'head'}, dimensions={1} | all-to-all | bytes 131072 | tf_op jit(solution)/shard_map/all_to_all | solution.py:349
  14.9 0.0 all-gather.2.cloned.1.call-update
  14.9 0.8 copy.12
  15.7 0.1 eq.15.picked_ref
  15.8 0.0 copy-start
  15.8 0.0 copy-start.1
  15.8 2.4 copy.13
  18.2 1.6 copy.14
  19.9 0.1 select_reduce_fusion.wanted_ref
  20.0 0.0 copy-done
  20.0 0.0 copy-done.1
  20.0 0.0 copy-start.2
  20.0 1.2 copy-done.2
  21.3 0.0 copy-start.3
  21.3 1.2 copy-done.3
  22.5 251.0 %shard_map.73 = bf16[2,512,1024]{2,1,0:T(8,128)(2,1)} custom-call(s32[128]{0:T(128)S(1)} %select_reduce_fusion.wanted_ref, s32[96]{0:T(128)S(1)} %eq.15.picked_ref, s32[1,128]{1,0:T(1,128)S(1)} %bitcast.12, bf16[512,1024]{1,0:T(8,128)(2,1)S(1)} %copy-done, bf16[512,1024]{1,0:T(8,128)(2,1)S(1)} %copy-done.1, bf16[512,1024]{1,0:T(8,128)(2,1)S(1)} %copy-done.2, ...), custom_call_target="tpu_custom_call" | custom-call | flops 6000000000 | bytes 700000000 | tf_op jit(solution)/shard_map/pallas_call | solution.py:304
  273.5 0.0 all-gather.2.cloned.1.call-done
  273.5 9.8 %bitcast_convert_fusion = bf16[512,2048]{1,0:T(8,128)(2,1)} fusion(bf16[2,512,1024]{2,1,0:T(8,128)(2,1)} %shard_map.73, bf16[2,1024,2048]{2,1,0:T(8,128)(2,1)} %all-gather.2.cloned.1.call-done), kind=kOutput, calls=%fused_computation | convolution fusion | flops 4296015872 | bytes 12582912 | tf_op jit(solution)/shard_map/gtr,grf->tf/dot_general | solution.py:357
  (1 shorter events, 0.0 us)
Async XLA Ops:
  6.5 267.0 %all-gather.2.cloned.1.call-start = ((), (), s32[]{:S(2)}) async-start(), calls=%async_computation.1 | async-start | bytes 8454144 | tf_op jit(solution)/shard_map/all_gather | solution.py:352
  15.8 4.2 %copy-start = (bf16[512,1024]{1,0:T(8,128)(2,1)S(1)}, bf16[512,1024]{1,0:T(8,128)(2,1)}, u32[]{:S(2)}) copy-start(bf16[512,1024]{1,0:T(8,128)(2,1)} %q_ref.1) | copy-start | bytes 3145732
  15.8 4.2 %copy-start.1 = (bf16[512,1024]{1,0:T(8,128)(2,1)S(1)}, bf16[512,1024]{1,0:T(8,128)(2,1)}, u32[]{:S(2)}) copy-start(bf16[512,1024]{1,0:T(8,128)(2,1)} %k_ref.1) | copy-start | bytes 3145732
  20.0 1.2 copy-start.2
  21.3 1.2 copy-start.3
Sparse Core Ops, SparseCore 0:
  15.0 205.7 all-gather.1

commit v2 on v1

--- a/solution.py
+++ b/solution.py
@@ -15,6 +15,8 @@
 TILES = 4
 HEADS = 8
 ITEMS = TILES * HEADS
+W_HALF = 1024
+CHUNK = 512
 NX, NZ, NY = 4, 8, 4
 PEERS = NX * NZ * NY
 SCALE2 = D_HEAD**-0.5 * math.log2(math.e)
@@ -69,15 +71,20 @@
     v_ref,
     pk_ref,
     pv_ref,
+    w_ref,
     out_ref,
     items,
     send_q,
     recv_q,
-    send_o,
     recv_o,
     send_l,
     recv_l,
+    kh,
     vt,
+    wbuf,
+    wmat,
+    att,
+    acc,
     own_o,
     own_l,
     table,
@@ -93,6 +100,10 @@
     t_recv_sem,
     h_send_sem,
     h_recv_sem,
+    s_send_sem,
+    s_recv_sem,
+    w_send_sem,
+    w_recv_sem,
 ):
     me = lax.axis_index("ctx")
     core = lax.axis_index("head")
@@ -133,9 +144,103 @@
             device_id_type=pl.DeviceIdType.MESH,
         )
 
+    def w_major(p):
+        return x if p == 0 else y
+
+    def w_minor(p):
+        return y if p == 0 else x
+
+    def w_device(p, major, minor, depth):
+        return place(major, depth, minor) if p == 0 else place(minor, depth, major)
+
+    def w_pos(p):
+        return (w_major(p) * NY + w_minor(p)) * NZ + z
+
+    def w_copy(p, slot, start, blocks, target):
+        return pltpu.make_async_remote_copy(
+            src_ref=wbuf.at[p, pl.ds(start, blocks)],
+            dst_ref=wbuf.at[p, pl.ds(start, blocks)],
+            send_sem=w_send_sem.at[p, slot],
+            recv_sem=w_recv_sem.at[p, slot],
+            device_id={"ctx": target},
+            device_id_type=pl.DeviceIdType.MESH,
+        )
+
+    def s_copy(p):
+        columns = pl.multiple_of((1 - core) * 2 * W_HALF + p * W_HALF, W_HALF)
+        return pltpu.make_async_remote_copy(
+            src_ref=w_ref.at[:, pl.ds(columns, W_HALF)],
+            dst_ref=wbuf.at[p, w_pos(p), core],
+            send_sem=s_send_sem.at[p],
+            recv_sem=s_recv_sem.at[p],
+            device_id={"head": 1 - core},
+            device_id_type=pl.DeviceIdType.MESH,
+        )
+
+    w_started = []
+
+    def w_send(p, slot, start, blocks, target):
+        c = w_copy(p, slot, start, blocks, target)
+        c.start()
+        w_started.append(c)
+
+    def w_line(p, level, ahead):
+        if level == 0:
+            minor = (w_minor(p) + ahead + 4) % 4
+            return (w_major(p) * 4 + minor) * NZ, w_device(p, w_major(p), minor, z)
+        major = (w_major(p) + ahead + 4) % 4
+        return major * 4 * NZ, w_device(p, major, w_minor(p), z)
+
+    def w_first(level):
+        blocks = (NZ, 4 * NZ)[level]
+        for p in range(2):
+            start = w_line(p, level, 0)[0]
+            w_send(p, 7 + 4 * level, start, blocks, w_line(p, level, 1)[1])
+            w_send(p, 8 + 4 * level, start, blocks, w_line(p, level, -1)[1])
+
+    def w_forward(level):
+        blocks = (NZ, 4 * NZ)[level]
+        half = blocks // 2
+        for p in range(2):
+            behind, ahead = w_line(p, level, -1), w_line(p, level, 1)
+            w_copy(p, 7 + 4 * level, behind[0], blocks, me).wait_recv()
+            w_send(p, 9 + 4 * level, behind[0], half, ahead[1])
+            w_copy(p, 8 + 4 * level, ahead[0], blocks, me).wait_recv()
+            w_send(p, 10 + 4 * level, ahead[0] + half, half, behind[1])
+
+    def w_settle(level):
+        half = (NZ, 4 * NZ)[level] // 2
+        for p in range(2):
+            opposite = w_line(p, level, 2)[0]
+            w_copy(p, 9 + 4 * level, opposite, half, me).wait_recv()
+            w_copy(p, 10 + 4 * level, opposite + half, half, me).wait_recv()
+
+    for p in range(2):
+        s_copy(p).start()
+        columns = pl.multiple_of(core * 2 * W_HALF + p * W_HALF, W_HALF)
+        wbuf[p, w_pos(p), core] = w_ref[:, pl.ds(columns, W_HALF)]
+
     y_copies = [table_copy(d - 1, 1, me, place(x, z, (y + d) % NY)) for d in range(1, NY)]
     for c in y_copies:
         c.start()
+
+    for p in range(2):
+        pltpu.make_async_remote_copy(
+            src_ref=w_ref.at[:, pl.ds(0, W_HALF)],
+            dst_ref=wbuf.at[p, w_pos(p), 1 - core],
+            send_sem=s_send_sem.at[p],
+            recv_sem=s_recv_sem.at[p],
+            device_id={"head": 1 - core},
+            device_id_type=pl.DeviceIdType.MESH,
+        ).wait_recv()
+        for d in range(1, NZ):
+            w_send(
+                p,
+                d - 1,
+                w_pos(p),
+                1,
+                w_device(p, w_major(p), w_minor(p), (z + d) % NZ),
+            )
 
     def q_copy(target, slot):
         return pltpu.make_async_remote_copy(
@@ -162,6 +267,11 @@
     for c in z_copies:
         c.start()
     lax.fori_loop(17, 49, send_query, 0)
+    for p in range(2):
+        base = w_pos(p) - z
+        for d in range(1, NZ):
+            w_copy(p, d - 1, base + (z - d + NZ) % NZ, 1, me).wait_recv()
+    w_first(0)
     for d in range(1, NZ):
         table_copy(2 + d, NY, place(x, (z - d + NZ) % NZ, 0), me).wait_recv()
     x_copies = [
@@ -171,6 +281,7 @@
     for c in x_copies:
         c.start()
     lax.fori_loop(49, PEERS, send_query, 0)
+    w_forward(0)
 
     for t in range(TILES):
         depth = (t + 1) * TILE
@@ -190,6 +301,9 @@
     for h in range(HEADS):
         columns = slice(h * D_HEAD, (h + 1) * D_HEAD)
         vt[h] = pv_ref[:, columns].T
+        kh[h] = pk_ref[:, columns]
+    w_settle(0)
+    w_first(1)
 
     for d in range(1, NX):
         table_copy(9 + d, NZ * NY, place((x - d + NX) % NX, 0, 0), me).wait_recv()
@@ -199,7 +313,7 @@
 
     def o_copy(target, slot):
         return pltpu.make_async_remote_copy(
-            src_ref=send_o.at[target],
+            src_ref=recv_q.at[target],
             dst_ref=recv_o.at[slot],
             send_sem=o_send_sem.at[target],
             recv_sem=o_recv_sem.at[slot],
@@ -219,7 +333,7 @@
 
     def answer(source, query):
         head = table_s[source, 0, me] % HEADS
-        return attend(pk_ref[head], vt[head], query)
+        return attend(kh[head], vt[head], query)
 
     out, lse = answer(me, items[wanted_ref[me]])
     recv_o[me] = out.astype(jnp.bfloat16)
@@ -229,13 +343,36 @@
         source = moved(me, step, -sign)
         q_copy(me, source).wait_recv()
         out, lse = answer(source, recv_q[source])
-        send_o[source] = out.astype(jnp.bfloat16)
+        recv_q[source] = out.astype(jnp.bfloat16)
         send_l[source] = lse
         o_copy(source, me).start()
         l_copy(source, me).start()
         return carry
 
-    lax.fori_loop(1, PEERS, serve, 0)
+    lax.fori_loop(1, 56, serve, 0)
+    w_forward(1)
+    lax.fori_loop(56, PEERS, serve, 0)
+
+    w_settle(1)
+
+    def in_order(pair, carry):
+        first = pair * 2
+        bx, bz, by = coords(first)
+        rows = pl.multiple_of(first * 8, 16)
+        for p in range(2):
+            if p == 0:
+                one = (bx * NY + by) * NZ + bz
+                two = one + NZ
+            else:
+                one = (by * NX + bx) * NZ + bz
+                two = one + NX * NZ
+            for g in range(2):
+                wmat[g, pl.ds(rows, 16), p * W_HALF : (p + 1) * W_HALF] = jnp.concatenate(
+                    [wbuf[p, one, g], wbuf[p, two, g]], axis=0
+                )
+        return carry
+
+    lax.fori_loop(0, PEERS // 2, in_order, 0)
 
     def settle(step, carry):
         server = moved(me, step, sign)
@@ -247,8 +384,8 @@
 
     def h_copy(t):
         return pltpu.make_async_remote_copy(
-            src_ref=out_ref.at[core, pl.ds(t * TILE, TILE)],
-            dst_ref=out_ref.at[core, pl.ds(t * TILE, TILE)],
+            src_ref=att.at[core, pl.ds(t * TILE, TILE)],
+            dst_ref=att.at[core, pl.ds(t * TILE, TILE)],
             send_sem=h_send_sem.at[t],
             recv_sem=h_recv_sem.at[t],
             device_id={"head": 1 - core},
@@ -267,21 +404,42 @@
             for f, s in zip(factors[1:], slots):
                 mixed = mixed + f * recv_o[s].astype(jnp.float32)
             mixed = mixed / total
-            out_ref[core, t * TILE : (t + 1) * TILE, h * D_HEAD : (h + 1) * D_HEAD] = (
+            att[core, t * TILE : (t + 1) * TILE, h * D_HEAD : (h + 1) * D_HEAD] = (
                 mixed.T.astype(jnp.bfloat16)
             )
         h_copy(t).start()
+
+    def project_own(chunk, carry):
+        columns = pl.ds(pl.multiple_of(chunk * CHUNK, CHUNK), CHUNK)
+        acc[:, columns] = jnp.dot(
+            att[core], wmat[core, :, columns], preferred_element_type=jnp.float32
+        )
+        return carry
+
+    lax.fori_loop(0, 2 * W_HALF // CHUNK, project_own, 0)
     for t in range(TILES):
         pltpu.make_async_remote_copy(
-            src_ref=out_ref.at[1 - core, pl.ds(t * TILE, TILE)],
-            dst_ref=out_ref.at[1 - core, pl.ds(t * TILE, TILE)],
+            src_ref=att.at[1 - core, pl.ds(t * TILE, TILE)],
+            dst_ref=att.at[1 - core, pl.ds(t * TILE, TILE)],
             send_sem=h_send_sem.at[t],
             recv_sem=h_recv_sem.at[t],
             device_id={"head": 1 - core},
             device_id_type=pl.DeviceIdType.MESH,
         ).wait_recv()
+
+    def project_other(chunk, carry):
+        columns = pl.ds(pl.multiple_of(chunk * CHUNK, CHUNK), CHUNK)
+        other = jnp.dot(
+            att[1 - core], wmat[1 - core, :, columns], preferred_element_type=jnp.float32
+        )
+        out_ref[:, columns] = (acc[:, columns] + other).astype(jnp.bfloat16)
+        return carry
+
+    lax.fori_loop(0, 2 * W_HALF // CHUNK, project_other, 0)
     for t in range(TILES):
         h_copy(t).wait_send()
+    for p in range(2):
+        s_copy(p).wait_send()
 
     def drain(step, carry):
         target = moved(me, step, sign)
@@ -292,29 +450,34 @@
         return carry
 
     lax.fori_loop(1, PEERS, drain, 0)
-    for c in y_copies + z_copies + x_copies:
+    for c in y_copies + z_copies + x_copies + w_started:
         c.wait_send()
 
 
-def attention_layer(wanted, picked, queries, keys, values, prefix_keys, prefix_values):
+def layer(wanted, picked, queries, keys, values, prefix_keys, prefix_values, weight):
     vmem = pl.BlockSpec(memory_space=pltpu.VMEM)
     smem = pl.BlockSpec(memory_space=pltpu.SMEM)
     slots = (PEERS, TILE, D_HEAD)
+    width = HEADS * D_HEAD
     sem = pltpu.SemaphoreType.DMA
     return pl.pallas_call(
         layer_kernel,
-        out_shape=jax.ShapeDtypeStruct((2, BLOCK, HEADS * D_HEAD), jnp.bfloat16),
-        in_specs=[smem, smem, vmem, vmem, vmem, vmem, vmem, vmem],
+        out_shape=jax.ShapeDtypeStruct((BLOCK, 2 * W_HALF), jnp.bfloat16),
+        in_specs=[smem, smem, vmem, vmem, vmem, vmem, vmem, vmem, vmem],
         out_specs=vmem,
         scratch_shapes=[
             pltpu.VMEM((ITEMS, TILE, D_HEAD), jnp.bfloat16),
             pltpu.VMEM(slots, jnp.bfloat16),
             pltpu.VMEM(slots, jnp.bfloat16),
             pltpu.VMEM(slots, jnp.bfloat16),
-            pltpu.VMEM(slots, jnp.bfloat16),
             pltpu.VMEM((PEERS, 1, TILE), jnp.float32),
             pltpu.VMEM((PEERS, 1, TILE), jnp.float32),
+            pltpu.VMEM((HEADS, BLOCK, D_HEAD), jnp.bfloat16),
             pltpu.VMEM((HEADS, D_HEAD, BLOCK), jnp.bfloat16),
+            pltpu.VMEM((2, PEERS, 2, 8, W_HALF), jnp.bfloat16),
+            pltpu.VMEM((2, width, 2 * W_HALF), jnp.bfloat16),
+            pltpu.VMEM((2, BLOCK, width), jnp.bfloat16),
+            pltpu.VMEM((BLOCK, 2 * W_HALF), jnp.float32),
             pltpu.VMEM((ITEMS, D_HEAD, TILE), jnp.float32),
             pltpu.VMEM((ITEMS, 1, TILE), jnp.float32),
             pltpu.VMEM((PEERS, 1, PEERS), jnp.int32),
@@ -330,14 +493,15 @@
             sem((13,)),
             sem((TILES,)),
             sem((TILES,)),
+            sem((2,)),
+            sem((2,)),
+            sem((2, 15)),
+            sem((2, 15)),
         ],
         compiler_params=pltpu.CompilerParams(
-            collective_id=0, has_side_effects=True, vmem_limit_bytes=48 * 1024 * 1024
+            collective_id=0, has_side_effects=True, vmem_limit_bytes=60 * 1024 * 1024
         ),
-        cost_estimate=pl.CostEstimate(
-            flops=6_000_000_000, bytes_accessed=700_000_000, transcendentals=10_000_000
-        ),
-    )(wanted, picked, wanted[None], queries, keys, values, prefix_keys, prefix_values)
+    )(wanted, picked, wanted[None], queries, keys, values, prefix_keys, prefix_values, weight)
 
 
 def shards(queries, keys, values, prefix_keys, prefix_values, selected, out_weight):
@@ -345,18 +509,9 @@
     matches = picked[None, :] == jnp.arange(PEERS, dtype=jnp.int32)[:, None]
     item_ids = jnp.arange(ITEMS * TOPK, dtype=jnp.int32) // TOPK
     wanted = jnp.sum(jnp.where(matches, item_ids[None, :], 0), axis=1)
-    features = out_weight.shape[2] // 2
-    swapped = lax.all_to_all(
-        out_weight[0].reshape(-1, 2, features), "head", split_axis=1, concat_axis=1, tiled=True
+    return layer(
+        wanted, picked, queries, keys, values, prefix_keys, prefix_values, out_weight[0]
     )
-    weight = lax.all_gather(swapped.transpose(1, 0, 2), "ctx", axis=1, tiled=True)
-    head_keys = prefix_keys.reshape(BLOCK, HEADS, D_HEAD).transpose(1, 0, 2)
-    attention = attention_layer(
-        wanted, picked, queries, keys, values, head_keys, prefix_values
-    )
-    return jnp.einsum(
-        "gtr,grf->tf", attention, weight, preferred_element_type=jnp.float32
-    ).astype(jnp.bfloat16)
 
 
 def solution(mesh):

time: 291 us -> 242 us (0.83)
  Pallas kernels: 251 us -> 237 us
  between operations: 13.5 us -> 0.02 us
  matrix products: 9.84 us -> 0 us
  blocking collectives: 8.33 us -> 0 us
  local copies, waits for them, and re-layouts: 7.41 us -> 4.05 us
    pallas_call x1, Pallas kernels: 251 us -> 237 us  [layer(): pl.pallas_call(layer_kernel, out_shape=jax.ShapeDtypeStruct((BLOCK, 2 * W...]
    dot_general x1 -> x0, matrix products: 9.84 us -> none  [shards(): jnp.einsum('gtr,grf->tf', attention, weight, preferred_element_type=jnp.f...]
    all_to_all x1 -> x0, blocking collectives: 8.33 us -> none  [shards(): lax.all_to_all(out_weight[0].reshape(-1, 2, features), 'head', split_axis...]
  transfers between devices with their start and end apart: 1 -> 0, of which waited for: 0 -> 0; matrix products, arithmetic and copies ran while one was open for 2% -> 0% of each run, Pallas kernels for 87% -> 0%
where the time goes in v2:
time: 242 us
  Pallas kernels  237 us (98%)
  local copies, waits for them, and re-layouts  4.05 us (2%)
    pallas_call x1, Pallas kernels, layer(): pl.pallas_call(layer_kernel, out_shape=jax.ShapeDtypeStruct((BLOCK, 2 * W...  237 us

profile of v2, /device:TPU:1, one launch (start us, length us, event | category | flops | bytes accessed | tf_op | source)
XLA Modules:
  0.0 242.0 jit_solution(2904824065079571573)
XLA Ops:
  0.0 0.8 copy.10
  0.8 0.1 eq.15.picked_ref
  0.9 0.0 copy-start
  0.9 0.6 select_reduce_fusion.wanted_ref
  1.5 0.0 copy-done
  1.5 237.3 %shard_map.73 = bf16[512,2048]{1,0:T(8,128)(2,1)} custom-call(s32[128]{0:T(128)} %select_reduce_fusion.wanted_ref, s32[96]{0:T(128)} %copy-done, s32[1,128]{1,0:T(1,128)} %bitcast.5, bf16[512,1024]{1,0:T(8,128)(2,1)} %q_ref.1, bf16[512,1024]{1,0:T(8,128)(2,1)} %k_ref.1, bf16[512,1024]{1,0:T(8,128)(2,1)} %v_ref.1, bf16[512,1024]{1,0:T(8,128)(2,1)} %pk_ref.1, ...), custom_call_target="tpu_custom_call" | custom-call | tf_op jit(solution)/shard_map/pallas_call | solution.py:463
  238.9 3.2 %copy.12 = bf16[512,2048]{1,0:T(8,128)(2,1)} copy(bf16[512,2048]{1,0:T(8,128)(2,1)} %shard_map.73) | data formatting | bytes 4194304
  (1 shorter events, 0.0 us)
Async XLA Ops:
  0.9 0.6 copy-start

commit v3 on v2

v3 whole, which is shorter than its diff:
```python
import functools
import math

import jax
import jax.numpy as jnp
from jax import lax
from jax.experimental import pallas as pl
from jax.experimental.pallas import tpu as pltpu
from jax.sharding import PartitionSpec as P

D_HEAD = 128
TILE = 128
BLOCK = 512
TOPK = 3
TILES = 4
HEADS = 8
ITEMS = TILES * HEADS
W_HALF = 1024
CHUNK = 512
TOGETHER = 3
NX, NZ, NY = 4, 8, 4
PEERS = NX * NZ * NY
PLANE = NX * NY
COLUMN = (0, -1, 1, -2, 2, -3, 3, 4)
SCALE2 = D_HEAD**-0.5 * math.log2(math.e)


def coords(index):
    return index // (NZ * NY), (index // NY) % NZ, index % NY


def place(x, z, y):
    return (x * NZ + z) * NY + y


def offset_of(step):
    dz = (step * 3) % NZ
    dy = (step // NZ) % NY
    dx = (step // (NZ * NY)) % NX
    return dx, dz, dy


def moved(me, step, sign):
    x, z, y = coords(me)
    dx, dz, dy = offset_of(step)
    return place((x + sign * dx + NX) % NX, (z + sign * dz + NZ) % NZ, (y + sign * dy + NY) % NY)


def attend(key_block, value_block_t, query, mask=None):
    scores = lax.dot_general(
        key_block, query, (((1,), (1,)), ((), ())), preferred_element_type=jnp.float32
    )
    scores = scores * SCALE2
    if mask is not None:
        scores = jnp.where(mask, scores, -jnp.inf)
    top = jnp.max(scores, axis=0, keepdims=True)
    weights = jnp.exp2(scores - top)
    total = jnp.sum(weights, axis=0, keepdims=True)
    out = lax.dot_general(
        value_block_t,
        weights.astype(jnp.bfloat16),
        (((1,), (0,)), ((), ())),
        preferred_element_type=jnp.float32,
    )
    return out / total, top + jnp.log2(total)


def layer_kernel(
    wanted_ref,
    picked_ref,
    wanted_row_ref,
    q_ref,
    k_ref,
    v_ref,
    pk_ref,
    pv_ref,
    w_ref,
    out_ref,
    items,
    up_one,
    up_two,
    down_one,
    down_two,
    onward,
    far,
    last,
    given,
    recv_q,
    recv_o,
    send_l,
    recv_l,
    kh,
    vt,
    wbuf,
    wmat,
    att,
    acc,
    own_o,
    own_l,
    table,
    column_s,
    table_s,
    table_sem,
    ring_send_sem,
    ring_recv_sem,
    q_send_sem,
    q_recv_sem,
    o_send_sem,
    o_recv_sem,
    l_send_sem,
    l_recv_sem,
    t_send_sem,
    t_recv_sem,
    h_send_sem,
    h_recv_sem,
    s_send_sem,
    s_recv_sem,
    w_send_sem,
    w_recv_sem,
):
    me = lax.axis_index("ctx")
    core = lax.axis_index("head")
    x, z, y = coords(me)
    sign = 1 - 2 * core
    near = ((up_one, up_two), (down_one, down_two))
    mesh = pl.DeviceIdType.MESH

    def depth(ahead):
        return (z + ahead + NZ) % NZ

    def remote(src, dst, send_sem, recv_sem, target):
        return pltpu.make_async_remote_copy(
            src_ref=src,
            dst_ref=dst,
            send_sem=send_sem,
            recv_sem=recv_sem,
            device_id={"ctx": target},
            device_id_type=mesh,
        )

    barrier = pltpu.get_barrier_semaphore()

    def greet(step, carry):
        pl.semaphore_signal(
            barrier, inc=1, device_id={"ctx": moved(me, step, 1)}, device_id_type=mesh
        )
        return carry

    lax.fori_loop(1, PEERS, greet, 0)
    pl.semaphore_signal(barrier, inc=1, device_id={"head": 1 - core}, device_id_type=mesh)

    for t in range(TILES):
        for h in range(HEADS):
            items[t * HEADS + h] = q_ref[
                t * TILE : (t + 1) * TILE, h * D_HEAD : (h + 1) * D_HEAD
            ]
    column_start = (x * NY + y) * NZ
    table[column_start + z] = wanted_row_ref[...]
    pl.semaphore_wait(barrier, PEERS)

    def ring(way, hop):
        if hop == 1:
            src, dst = items, near[way][0]
        elif hop == 2:
            src, dst = near[way][0], near[way][1]
        elif hop == 3:
            src, dst = onward.at[way], far.at[way]
        else:
            src, dst = far.at[way, pl.ds(PLANE, PLANE // 2)], last.at[
                pl.ds(way * (PLANE // 2), PLANE // 2)
            ]
        return remote(
            src,
            dst,
            ring_send_sem.at[way, hop - 1],
            ring_recv_sem.at[way, hop - 1],
            place(x, depth(1 - 2 * way), y),
        )

    started = []

    def start(copy):
        copy.start()
        started.append(copy)

    def w_major(p):
        return x if p == 0 else y

    def w_minor(p):
        return y if p == 0 else x

    def w_device(p, major, minor):
        return place(major, z, minor) if p == 0 else place(minor, z, major)

    def w_column(p):
        return (w_major(p) * NY + w_minor(p)) * NZ

    def w_copy(p, slot, first, blocks, target):
        return remote(
            wbuf.at[p, pl.ds(first, blocks)],
            wbuf.at[p, pl.ds(first, blocks)],
            w_send_sem.at[p, slot],
            w_recv_sem.at[p, slot],
            target,
        )

    def s_copy(p, group):
        columns = pl.multiple_of((1 - core) * 2 * W_HALF + p * W_HALF, W_HALF)
        return pltpu.make_async_remote_copy(
            src_ref=w_ref.at[:, pl.ds(columns, W_HALF)],
            dst_ref=wbuf.at[p, w_column(p) + z, group],
            send_sem=s_send_sem.at[p],
            recv_sem=s_recv_sem.at[p],
            device_id={"head": 1 - core},
            device_id_type=mesh,
        )

    def w_ways(hop, p):
        return (0, 1) if hop < 4 else (p,)

    def w_hop(hop):
        for p in range(2):
            for way in w_ways(hop, p):
                ahead = 1 - 2 * way
                block = w_column(p) + depth(-ahead * (hop - 1))
                start(w_copy(p, 2 * hop - 2 + way, block, 1, place(x, depth(ahead), y)))

    def w_hop_wait(hop):
        for p in range(2):
            for way in w_ways(hop, p):
                block = w_column(p) + depth(-(1 - 2 * way) * hop)
                w_copy(p, 2 * hop - 2 + way, block, 1, me).wait_recv()

    def w_line(p, level, ahead):
        if level == 0:
            minor = (w_minor(p) + ahead + 4) % 4
            return (w_major(p) * 4 + minor) * NZ, w_device(p, w_major(p), minor)
        major = (w_major(p) + ahead + 4) % 4
        return major * 4 * NZ, w_device(p, major, w_minor(p))

    def w_first(level):
        blocks = (NZ, 4 * NZ)[level]
        for p in range(2):
            first = w_line(p, level, 0)[0]
            start(w_copy(p, 8 + 4 * level, first, blocks, w_line(p, level, 1)[1]))
            start(w_copy(p, 9 + 4 * level, first, blocks, w_line(p, level, -1)[1]))

    def w_forward(level):
        blocks = (NZ, 4 * NZ)[level]
        half = blocks // 2
        for p in range(2):
            behind, ahead = w_line(p, level, -1), w_line(p, level, 1)
            w_copy(p, 8 + 4 * level, behind[0], blocks, me).wait_recv()
            start(w_copy(p, 10 + 4 * level, behind[0], half, ahead[1]))
            w_copy(p, 9 + 4 * level, ahead[0], blocks, me).wait_recv()
            start(w_copy(p, 11 + 4 * level, ahead[0] + half, half, behind[1]))

    def w_settle(level):
        half = (NZ, 4 * NZ)[level] // 2
        for p in range(2):
            opposite = w_line(p, level, 2)[0]
            w_copy(p, 10 + 4 * level, opposite, half, me).wait_recv()
            w_copy(p, 11 + 4 * level, opposite + half, half, me).wait_recv()

    def table_copy(slot, first, rows, target):
        return remote(
            table.at[pl.ds(first, rows)],
            table.at[pl.ds(first, rows)],
            t_send_sem.at[slot],
            t_recv_sem.at[slot],
            target,
        )

    for way in range(2):
        start(ring(way, 1))
    for p in range(2):
        s_copy(p, core).start()
        columns = pl.multiple_of(core * 2 * W_HALF + p * W_HALF, W_HALF)
        wbuf[p, w_column(p) + z, core] = w_ref[:, pl.ds(columns, W_HALF)]
    for d in range(1, NZ):
        start(table_copy(d - 1, column_start + z, 1, place(x, depth(d), y)))

    def in_plane(step, way):
        return (x + way * (step // NY) + NX) % NX, (y + way * (step % NY) + NY) % NY

    def q_copy(src, number, member, source, target):
        return remote(
            src, recv_q.at[source], q_send_sem.at[number, member], q_recv_sem.at[source], target
        )

    def hand_out(number, read, keep):
        source = place(x, depth(COLUMN[number]), y)

        def give(step, carry):
            tx, ty = in_plane(step, sign)
            member = tx * NY + ty
            target = place(tx, z, ty)
            q_copy(read(member, target), number, member, source, target).start()
            return carry

        lax.fori_loop(1, PLANE, give, 0)
        recv_q[source] = keep()

    def hand_out_tiles(number, tiles, row_of):
        def read(member, target):
            given[number, member] = tiles[row_of(target)]
            return given.at[number, member]

        hand_out(number, read, lambda: tiles[row_of(me)])

    def column_row(ahead):
        row = depth(ahead)
        return lambda target: column_s[row, 0, target]

    hand_out_tiles(0, items, lambda target: wanted_ref[target])

    for p in range(2):
        s_copy(p, 1 - core).wait_recv()
    w_hop(1)

    for d in range(1, NZ):
        table_copy(d - 1, column_start + depth(-d), 1, me).wait_recv()
    to_scalars = pltpu.make_async_copy(table.at[pl.ds(column_start, NZ)], column_s, table_sem)
    to_scalars.start()
    to_scalars.wait()
    for d in range(1, NY):
        start(table_copy(6 + d, column_start, NZ, place(x, z, (y + d) % NY)))

    def own_tile(t):
        keys_seen = (t + 1) * TILE
        row = lax.broadcasted_iota(jnp.int32, (keys_seen, TILE), 0)
        column = lax.broadcasted_iota(jnp.int32, (keys_seen, TILE), 1)
        mask = row <= column + t * TILE
        for h in range(HEADS):
            columns = slice(h * D_HEAD, (h + 1) * D_HEAD)
            out, lse = attend(
                k_ref[:keys_seen, columns],
                v_ref[:keys_seen, columns].T,
                q_ref[t * TILE : (t + 1) * TILE, columns],
                mask,
            )
            own_o[t * HEADS + h] = out
            own_l[t * HEADS + h] = lse

    for h in range(HEADS):
        columns = slice(h * D_HEAD, (h + 1) * D_HEAD)
        vt[h] = pv_ref[:, columns].T
        kh[h] = pk_ref[:, columns]
    for d in range(1, NY):
        table_copy(6 + d, (x * NY + (y - d + NY) % NY) * NZ, NZ, me).wait_recv()
    for d in range(1, NX):
        start(table_copy(9 + d, x * NY * NZ, NY * NZ, place((x + d) % NX, z, y)))
    for t in range(TILES):
        own_tile(t)
    for d in range(1, NX):
        table_copy(9 + d, (x - d + NX) % NX * NY * NZ, NY * NZ, me).wait_recv()
    to_scalars = pltpu.make_async_copy(table, table_s, table_sem)
    to_scalars.start()
    to_scalars.wait()

    def o_copy(target, slot):
        return remote(
            recv_q.at[target], recv_o.at[slot], o_send_sem.at[target], o_recv_sem.at[slot], target
        )

    def l_copy(target, slot):
        return remote(
            send_l.at[target], recv_l.at[slot], l_send_sem.at[target], l_recv_sem.at[slot], target
        )

    def answer(source):
        sx, sz, sy = coords(source)
        head = table_s[(sx * NY + sy) * NZ + sz, 0, me] % HEADS
        return attend(kh[head], vt[head], recv_q[source])

    def reply(source, found):
        recv_q[source] = found[0].astype(jnp.bfloat16)
        send_l[source] = found[1]
        o_copy(source, me).start()
        l_copy(source, me).start()

    def serve(number):
        ahead = COLUMN[number]
        plane = depth(ahead)
        if ahead == 0:
            out, lse = answer(me)
            recv_o[me] = out.astype(jnp.bfloat16)
            recv_l[me] = lse
        else:
            reply(place(x, plane, y), answer(place(x, plane, y)))

        def several(turn, carry):
            sources = []
            for j in range(TOGETHER):
                sx, sy = in_plane(1 + turn * TOGETHER + j, -sign)
                sources.append(place(sx, plane, sy))
            for source in sources:
                q_copy(given.at[0, 0], 0, 0, source, me).wait_recv()
            found = [answer(source) for source in sources]
            for source, one in zip(sources, found):
                reply(source, one)
            return carry

        lax.fori_loop(0, (PLANE - 1) // TOGETHER, several, 0)

    serve(0)

    for way in range(2):
        ring(way, 1).wait_recv()
        start(ring(way, 2))
    w_hop_wait(1)
    w_hop(2)
    for way in range(2):
        hand_out_tiles(1 + way, near[way][0], column_row(2 * way - 1))
    serve(1)
    serve(2)

    for way in range(2):
        ahead = 1 - 2 * way
        ring(way, 2).wait_recv()
        row_of = column_row(-2 * ahead)

        def build(member, carry, way=way, ahead=ahead, row_of=row_of):
            target = place(member // NY, depth(ahead), member % NY)
            onward[way, member] = near[way][1][row_of(target)]
            return carry

        def build_behind(member, carry, way=way, ahead=ahead, row_of=row_of):
            other = member + way * (PLANE // 2)
            target = place(other // NY, depth(2 * ahead), other % NY)
            onward[way, PLANE + member] = near[way][1][row_of(target)]
            return carry

        lax.fori_loop(0, PLANE, build, 0)
        lax.fori_loop(0, PLANE // 2, build_behind, 0)
        start(ring(way, 3))
    w_hop_wait(2)
    w_hop(3)
    for way in range(2):
        hand_out_tiles(3 + way, near[way][1], column_row(2 * (2 * way - 1)))
    serve(3)
    serve(4)

    here = x * NY + y
    for way in range(2):
        ring(way, 3).wait_recv()
        start(ring(way, 4))
    w_hop_wait(3)
    w_hop(4)
    for way in range(2):
        hand_out(
            5 + way, lambda member, target, way=way: far.at[way, member], lambda way=way: far[way, here]
        )
    serve(5)
    serve(6)

    for way in range(2):
        ring(way, 4).wait_recv()
    w_hop_wait(4)
    w_first(0)
    hand_out(7, lambda member, target: last.at[member], lambda: last[here])
    w_forward(0)
    serve(7)
    w_settle(0)
    w_first(1)
    w_forward(1)
    w_settle(1)

    def in_order(pair, carry):
        first = pair * 2
        bx, bz, by = coords(first)
        rows = pl.multiple_of(first * 8, 16)
        for p in range(2):
            if p == 0:
                one = (bx * NY + by) * NZ + bz
                two = one + NZ
            else:
                one = (by * NX + bx) * NZ + bz
                two = one + NX * NZ
            for g in range(2):
                wmat[g, pl.ds(rows, 16), p * W_HALF : (p + 1) * W_HALF] = jnp.concatenate(
                    [wbuf[p, one, g], wbuf[p, two, g]], axis=0
                )
        return carry

    lax.fori_loop(0, PEERS // 2, in_order, 0)

    def settle(step, carry):
        server = moved(me, step, sign)
        o_copy(me, server).wait_recv()
        l_copy(me, server).wait_recv()
        return carry

    lax.fori_loop(1, PEERS, settle, 0)

    def h_copy(t, group):
        return pltpu.make_async_remote_copy(
            src_ref=att.at[group, pl.ds(t * TILE, TILE)],
            dst_ref=att.at[group, pl.ds(t * TILE, TILE)],
            send_sem=h_send_sem.at[t],
            recv_sem=h_recv_sem.at[t],
            device_id={"head": 1 - core},
            device_id_type=mesh,
        )

    for t in range(TILES):
        for h in range(HEADS):
            item = t * HEADS + h
            slots = [picked_ref[item * TOPK + j] for j in range(TOPK)]
            lses = [own_l[item]] + [recv_l[s] for s in slots]
            highest = functools.reduce(jnp.maximum, lses)
            factors = [jnp.exp2(v - highest) for v in lses]
            total = functools.reduce(jnp.add, factors)
            mixed = factors[0] * own_o[item]
            for f, s in zip(factors[1:], slots):
                mixed = mixed + f * recv_o[s].astype(jnp.float32)
            mixed = mixed / total
            att[core, t * TILE : (t + 1) * TILE, h * D_HEAD : (h + 1) * D_HEAD] = mixed.T.astype(
                jnp.bfloat16
            )
        h_copy(t, core).start()

    def project_own(chunk, carry):
        columns = pl.ds(pl.multiple_of(chunk * CHUNK, CHUNK), CHUNK)
        acc[:, columns] = jnp.dot(
            att[core], wmat[core, :, columns], preferred_element_type=jnp.float32
        )
        return carry

    lax.fori_loop(0, 2 * W_HALF // CHUNK, project_own, 0)
    for t in range(TILES):
        h_copy(t, 1 - core).wait_recv()

    def project_other(chunk, carry):
        columns = pl.ds(pl.multiple_of(chunk * CHUNK, CHUNK), CHUNK)
        other = jnp.dot(
            att[1 - core], wmat[1 - core, :, columns], preferred_element_type=jnp.float32
        )
        out_ref[:, columns] = (acc[:, columns] + other).astype(jnp.bfloat16)
        return carry

    lax.fori_loop(0, 2 * W_HALF // CHUNK, project_other, 0)

    for t in range(TILES):
        h_copy(t, core).wait_send()
    for p in range(2):
        s_copy(p, core).wait_send()
    for number in range(NZ):

        def drain_slots(step, carry, number=number):
            tx, ty = in_plane(step, sign)
            q_copy(given.at[0, 0], number, tx * NY + ty, me, me).wait_send()
            return carry

        lax.fori_loop(1, PLANE, drain_slots, 0)

    def drain(step, carry):
        source = moved(me, step, -sign)
        o_copy(source, me).wait_send()
        l_copy(source, me).wait_send()
        return carry

    lax.fori_loop(1, PEERS, drain, 0)
    for copy in started:
        copy.wait_send()


def layer(wanted, picked, queries, keys, values, prefix_keys, prefix_values, weight):
    vmem = pl.BlockSpec(memory_space=pltpu.VMEM)
    smem = pl.BlockSpec(memory_space=pltpu.SMEM)
    slots = (PEERS, TILE, D_HEAD)
    width = HEADS * D_HEAD
    sem = pltpu.SemaphoreType.DMA
    return pl.pallas_call(
        layer_kernel,
        out_shape=jax.ShapeDtypeStruct((BLOCK, 2 * W_HALF), jnp.bfloat16),
        in_specs=[smem, smem, vmem, vmem, vmem, vmem, vmem, vmem, vmem],
        out_specs=vmem,
        scratch_shapes=[
            pltpu.VMEM((ITEMS, TILE, D_HEAD), jnp.bfloat16),
            pltpu.VMEM((ITEMS, TILE, D_HEAD), jnp.bfloat16),
            pltpu.VMEM((ITEMS, TILE, D_HEAD), jnp.bfloat16),
            pltpu.VMEM((ITEMS, TILE, D_HEAD), jnp.bfloat16),
            pltpu.VMEM((ITEMS, TILE, D_HEAD), jnp.bfloat16),
            pltpu.VMEM((2, 3 * PLANE // 2, TILE, D_HEAD), jnp.bfloat16),
            pltpu.VMEM((2, 3 * PLANE // 2, TILE, D_HEAD), jnp.bfloat16),
            pltpu.VMEM((PLANE, TILE, D_HEAD), jnp.bfloat16),
            pltpu.VMEM((5, PLANE, TILE, D_HEAD), jnp.bfloat16),
            pltpu.VMEM(slots, jnp.bfloat16),
            pltpu.VMEM(slots, jnp.bfloat16),
            pltpu.VMEM((PEERS, 1, TILE), jnp.float32),
            pltpu.VMEM((PEERS, 1, TILE), jnp.float32),
            pltpu.VMEM((HEADS, BLOCK, D_HEAD), jnp.bfloat16),
            pltpu.VMEM((HEADS, D_HEAD, BLOCK), jnp.bfloat16),
            pltpu.VMEM((2, PEERS, 2, 8, W_HALF), jnp.bfloat16),
            pltpu.VMEM((2, width, 2 * W_HALF), jnp.bfloat16),
            pltpu.VMEM((2, BLOCK, width), jnp.bfloat16),
            pltpu.VMEM((BLOCK, 2 * W_HALF), jnp.float32),
            pltpu.VMEM((ITEMS, D_HEAD, TILE), jnp.float32),
            pltpu.VMEM((ITEMS, 1, TILE), jnp.float32),
            pltpu.VMEM((PEERS, 1, PEERS), jnp.int32),
            pltpu.SMEM((NZ, 1, PEERS), jnp.int32),
            pltpu.SMEM((PEERS, 1, PEERS), jnp.int32),
            sem,
            sem((2, 4)),
            sem((2, 4)),
            sem((NZ, PLANE)),
            sem((PEERS,)),
            sem((PEERS,)),
            sem((PEERS,)),
            sem((PEERS,)),
            sem((PEERS,)),
            sem((13,)),
            sem((13,)),
            sem((TILES,)),
            sem((TILES,)),
            sem((2,)),
            sem((2,)),
            sem((2, 16)),
            sem((2, 16)),
        ],
        compiler_params=pltpu.CompilerParams(
            collective_id=0, has_side_effects=True, vmem_limit_bytes=60 * 1024 * 1024
        ),
    )(wanted, picked, wanted[None], queries, keys, values, prefix_keys, prefix_values, weight)


def shards(queries, keys, values, prefix_keys, prefix_values, selected, out_weight):
    picked = selected.reshape(ITEMS * TOPK)
    matches = picked[None, :] == jnp.arange(PEERS, dtype=jnp.int32)[:, None]
    item_ids = jnp.arange(ITEMS * TOPK, dtype=jnp.int32) // TOPK
    wanted = jnp.sum(jnp.where(matches, item_ids[None, :], 0), axis=1)
    return layer(
        wanted, picked, queries, keys, values, prefix_keys, prefix_values, out_weight[0]
    )


def solution(mesh):
    return jax.shard_map(
        shards,
        mesh=mesh,
        in_specs=(
            P("ctx", "head"),
            P("ctx", "head"),
            P("ctx", "head"),
            P("ctx", "head"),
            P("ctx", "head"),
            P("head", "ctx", None, None),
            P("head", "ctx", None),
        ),
        out_specs=P("ctx", "head"),
        check_vma=False,
    )
```

time: 242 us -> 248 us (1.025)
  Pallas kernels: 237 us -> 243 us
    pallas_call x1, Pallas kernels: 237 us -> 243 us  [layer(): pl.pallas_call(layer_kernel, out_shape=jax.ShapeDtypeStruct((BLOCK, 2 * W...]
where the time goes in v3:
time: 248 us; the launch traced here: 247 us
  Pallas kernels  243 us (98%)
  local copies, waits for them, and re-layouts  4.05 us (2%)
    pallas_call x1, Pallas kernels, layer(): pl.pallas_call(layer_kernel, out_shape=jax.ShapeDtypeStruct((BLOCK, 2 * W...  243 us

profile of v3, /device:TPU:1, one launch (start us, length us, event | category | flops | bytes accessed | tf_op | source)
XLA Modules:
  0.0 247.5 jit_solution(16200593733084400519)
XLA Ops:
  0.0 0.8 copy.10
  0.8 0.1 eq.15.picked_ref
  0.9 0.0 copy-start
  0.9 0.6 select_reduce_fusion.wanted_ref
  1.5 0.0 copy-done
  1.5 242.8 %shard_map.73 = bf16[512,2048]{1,0:T(8,128)(2,1)} custom-call(s32[128]{0:T(128)} %select_reduce_fusion.wanted_ref, s32[96]{0:T(128)} %copy-done, s32[1,128]{1,0:T(1,128)} %bitcast.5, bf16[512,1024]{1,0:T(8,128)(2,1)} %q_ref.1, bf16[512,1024]{1,0:T(8,128)(2,1)} %k_ref.1, bf16[512,1024]{1,0:T(8,128)(2,1)} %v_ref.1, bf16[512,1024]{1,0:T(8,128)(2,1)} %pk_ref.1, ...), custom_call_target="tpu_custom_call" | custom-call | tf_op jit(solution)/shard_map/pallas_call | solution.py:574
  244.3 3.2 %copy.12 = bf16[512,2048]{1,0:T(8,128)(2,1)} copy(bf16[512,2048]{1,0:T(8,128)(2,1)} %shard_map.73) | data formatting | bytes 4194304
  (1 shorter events, 0.0 us)
Async XLA Ops:
  0.9 0.6 copy-start

commit v4 on v2

--- a/solution.py
+++ b/solution.py
@@ -59,7 +59,7 @@
         (((1,), (0,)), ((), ())),
         preferred_element_type=jnp.float32,
     )
-    return out / total, top + jnp.log2(total)
+    return out * (1.0 / total), top + jnp.log2(total)
 
 
 def layer_kernel(
@@ -195,25 +195,25 @@
         blocks = (NZ, 4 * NZ)[level]
         for p in range(2):
             start = w_line(p, level, 0)[0]
-            w_send(p, 7 + 4 * level, start, blocks, w_line(p, level, 1)[1])
-            w_send(p, 8 + 4 * level, start, blocks, w_line(p, level, -1)[1])
+            w_send(p, 8 + 4 * level, start, blocks, w_line(p, level, 1)[1])
+            w_send(p, 9 + 4 * level, start, blocks, w_line(p, level, -1)[1])
 
     def w_forward(level):
         blocks = (NZ, 4 * NZ)[level]
         half = blocks // 2
         for p in range(2):
             behind, ahead = w_line(p, level, -1), w_line(p, level, 1)
-            w_copy(p, 7 + 4 * level, behind[0], blocks, me).wait_recv()
-            w_send(p, 9 + 4 * level, behind[0], half, ahead[1])
-            w_copy(p, 8 + 4 * level, ahead[0], blocks, me).wait_recv()
-            w_send(p, 10 + 4 * level, ahead[0] + half, half, behind[1])
+            w_copy(p, 8 + 4 * level, behind[0], blocks, me).wait_recv()
+            w_send(p, 10 + 4 * level, behind[0], half, ahead[1])
+            w_copy(p, 9 + 4 * level, ahead[0], blocks, me).wait_recv()
+            w_send(p, 11 + 4 * level, ahead[0] + half, half, behind[1])
 
     def w_settle(level):
         half = (NZ, 4 * NZ)[level] // 2
         for p in range(2):
             opposite = w_line(p, level, 2)[0]
-            w_copy(p, 9 + 4 * level, opposite, half, me).wait_recv()
-            w_copy(p, 10 + 4 * level, opposite + half, half, me).wait_recv()
+            w_copy(p, 10 + 4 * level, opposite, half, me).wait_recv()
+            w_copy(p, 11 + 4 * level, opposite + half, half, me).wait_recv()
 
     for p in range(2):
         s_copy(p).start()
@@ -224,6 +224,47 @@
     for c in y_copies:
         c.start()
 
+    def w_ways(hop, p):
+        return (0, 1) if hop < 4 else (p,)
+
+    def w_block(p, ahead):
+        return w_pos(p) - z + (z + ahead + NZ) % NZ
+
+    def w_hop(hop):
+        for p in range(2):
+            for way in w_ways(hop, p):
+                ahead = 1 - 2 * way
+                w_send(
+                    p,
+                    2 * hop - 2 + way,
+                    w_block(p, -ahead * (hop - 1)),
+                    1,
+                    place(x, (z + ahead + NZ) % NZ, y),
+                )
+
+    def w_hop_wait(hop):
+        for p in range(2):
+            for way in w_ways(hop, p):
+                block = w_block(p, -(1 - 2 * way) * hop)
+                w_copy(p, 2 * hop - 2 + way, block, 1, me).wait_recv()
+
+    def q_copy(target, slot):
+        return pltpu.make_async_remote_copy(
+            src_ref=send_q.at[target],
+            dst_ref=recv_q.at[slot],
+            send_sem=q_send_sem.at[target],
+            recv_sem=q_recv_sem.at[slot],
+            device_id={"ctx": target},
+            device_id_type=pl.DeviceIdType.MESH,
+        )
+
+    def send_query(step, carry):
+        target = moved(me, step, sign)
+        send_q[target] = items[wanted_ref[target]]
+        q_copy(target, me).start()
+        return carry
+
+    lax.fori_loop(1, 17, send_query, 0)
     for p in range(2):
         pltpu.make_async_remote_copy(
             src_ref=w_ref.at[:, pl.ds(0, W_HALF)],
@@ -233,32 +274,7 @@
             device_id={"head": 1 - core},
             device_id_type=pl.DeviceIdType.MESH,
         ).wait_recv()
-        for d in range(1, NZ):
-            w_send(
-                p,
-                d - 1,
-                w_pos(p),
-                1,
-                w_device(p, w_major(p), w_minor(p), (z + d) % NZ),
-            )
-
-    def q_copy(target, slot):
-        return pltpu.make_async_remote_copy(
-            src_ref=send_q.at[target],
-            dst_ref=recv_q.at[slot],
-            send_sem=q_send_sem.at[target],
-            recv_sem=q_recv_sem.at[slot],
-            device_id={"ctx": target},
-            device_id_type=pl.DeviceIdType.MESH,
-        )
-
-    def send_query(step, carry):
-        target = moved(me, step, sign)
-        send_q[target] = items[wanted_ref[target]]
-        q_copy(target, me).start()
-        return carry
-
-    lax.fori_loop(1, 17, send_query, 0)
+    w_hop(1)
     for d in range(1, NY):
         table_copy(d - 1, 1, place(x, z, (y - d + NY) % NY), me).wait_recv()
     z_copies = [
@@ -267,11 +283,8 @@
     for c in z_copies:
         c.start()
     lax.fori_loop(17, 49, send_query, 0)
-    for p in range(2):
-        base = w_pos(p) - z
-        for d in range(1, NZ):
-            w_copy(p, d - 1, base + (z - d + NZ) % NZ, 1, me).wait_recv()
-    w_first(0)
+    w_hop_wait(1)
+    w_hop(2)
     for d in range(1, NZ):
         table_copy(2 + d, NY, place(x, (z - d + NZ) % NZ, 0), me).wait_recv()
     x_copies = [
@@ -281,7 +294,6 @@
     for c in x_copies:
         c.start()
     lax.fori_loop(49, PEERS, send_query, 0)
-    w_forward(0)
 
     for t in range(TILES):
         depth = (t + 1) * TILE
@@ -298,12 +310,18 @@
             )
             own_o[t * HEADS + h] = out
             own_l[t * HEADS + h] = lse
+        if t == 1:
+            w_hop_wait(2)
+            w_hop(3)
+        elif t == 2:
+            w_hop_wait(3)
+            w_hop(4)
     for h in range(HEADS):
         columns = slice(h * D_HEAD, (h + 1) * D_HEAD)
         vt[h] = pv_ref[:, columns].T
         kh[h] = pk_ref[:, columns]
-    w_settle(0)
-    w_first(1)
+    w_hop_wait(4)
+    w_first(0)
 
     for d in range(1, NX):
         table_copy(9 + d, NZ * NY, place((x - d + NX) % NX, 0, 0), me).wait_recv()
@@ -349,9 +367,14 @@
         l_copy(source, me).start()
         return carry
 
-    lax.fori_loop(1, 56, serve, 0)
+    lax.fori_loop(1, 9, serve, 0)
+    w_forward(0)
+    lax.fori_loop(9, 17, serve, 0)
+    w_settle(0)
+    w_first(1)
+    lax.fori_loop(17, 80, serve, 0)
     w_forward(1)
-    lax.fori_loop(56, PEERS, serve, 0)
+    lax.fori_loop(80, PEERS, serve, 0)
 
     w_settle(1)
 
@@ -400,10 +423,10 @@
             highest = functools.reduce(jnp.maximum, lses)
             factors = [jnp.exp2(v - highest) for v in lses]
             total = functools.reduce(jnp.add, factors)
+            factors = [f * (1.0 / total) for f in factors]
             mixed = factors[0] * own_o[item]
             for f, s in zip(factors[1:], slots):
                 mixed = mixed + f * recv_o[s].astype(jnp.float32)
-            mixed = mixed / total
             att[core, t * TILE : (t + 1) * TILE, h * D_HEAD : (h + 1) * D_HEAD] = (
                 mixed.T.astype(jnp.bfloat16)
             )
@@ -495,8 +518,8 @@
             sem((TILES,)),
             sem((2,)),
             sem((2,)),
-            sem((2, 15)),
-            sem((2, 15)),
+            sem((2, 16)),
+            sem((2, 16)),
         ],
         compiler_params=pltpu.CompilerParams(
             collective_id=0, has_side_effects=True, vmem_limit_bytes=60 * 1024 * 1024

time: 242 us -> 242 us (level)
  no operation moved by 1% of the time
where the time goes in v4:
time: 242 us
  Pallas kernels  237 us (98%)
  local copies, waits for them, and re-layouts  4.05 us (2%)
    pallas_call x1, Pallas kernels, layer(): pl.pallas_call(layer_kernel, out_shape=jax.ShapeDtypeStruct((BLOCK, 2 * W...  237 us

profile of v4, /device:TPU:1, one launch (start us, length us, event | category | flops | bytes accessed | tf_op | source)
XLA Modules:
  0.0 242.1 jit_solution(49495055342275706)
XLA Ops:
  0.0 0.8 copy.10
  0.8 0.1 eq.15.picked_ref
  0.9 0.0 copy-start
  0.9 0.6 select_reduce_fusion.wanted_ref
  1.5 0.0 copy-done
  1.5 237.4 %shard_map.73 = bf16[512,2048]{1,0:T(8,128)(2,1)} custom-call(s32[128]{0:T(128)} %select_reduce_fusion.wanted_ref, s32[96]{0:T(128)} %copy-done, s32[1,128]{1,0:T(1,128)} %bitcast.5, bf16[512,1024]{1,0:T(8,128)(2,1)} %q_ref.1, bf16[512,1024]{1,0:T(8,128)(2,1)} %k_ref.1, bf16[512,1024]{1,0:T(8,128)(2,1)} %v_ref.1, bf16[512,1024]{1,0:T(8,128)(2,1)} %pk_ref.1, ...), custom_call_target="tpu_custom_call" | custom-call | tf_op jit(solution)/shard_map/pallas_call | solution.py:486
  239.0 3.2 %copy.12 = bf16[512,2048]{1,0:T(8,128)(2,1)} copy(bf16[512,2048]{1,0:T(8,128)(2,1)} %shard_map.73) | data formatting | bytes 4194304
  (1 shorter events, 0.0 us)
Async XLA Ops:
  0.9 0.6 copy-start

commit v5 on v4

--- a/solution.py
+++ b/solution.py
@@ -372,12 +372,6 @@
     lax.fori_loop(9, 17, serve, 0)
     w_settle(0)
     w_first(1)
-    lax.fori_loop(17, 80, serve, 0)
-    w_forward(1)
-    lax.fori_loop(80, PEERS, serve, 0)
-
-    w_settle(1)
-
     def in_order(pair, carry):
         first = pair * 2
         bx, bz, by = coords(first)
@@ -395,7 +389,13 @@
                 )
         return carry
 
+    lax.fori_loop(17, 56, serve, 0)
+    w_forward(1)
+    lax.fori_loop(56, 76, serve, 0)
+    w_settle(1)
     lax.fori_loop(0, PEERS // 2, in_order, 0)
+    lax.fori_loop(76, PEERS, serve, 0)
+
 
     def settle(step, carry):
         server = moved(me, step, sign)

time: 242 us -> 256 us (1.058)
  Pallas kernels: 237 us -> 251 us
    pallas_call x1, Pallas kernels: 237 us -> 251 us  [layer(): pl.pallas_call(layer_kernel, out_shape=jax.ShapeDtypeStruct((BLOCK, 2 * W...]
where the time goes in v5:
time: 256 us
  Pallas kernels  251 us (98%)
  local copies, waits for them, and re-layouts  4.05 us (2%)
    pallas_call x1, Pallas kernels, layer(): pl.pallas_call(layer_kernel, out_shape=jax.ShapeDtypeStruct((BLOCK, 2 * W...  251 us

profile of v5, /device:TPU:1, one launch (start us, length us, event | category | flops | bytes accessed | tf_op | source)
XLA Modules:
  0.0 255.8 jit_solution(17263029787943433620)
XLA Ops:
  0.0 0.8 copy.10
  0.8 0.1 eq.15.picked_ref
  0.9 0.0 copy-start
  0.9 0.6 select_reduce_fusion.wanted_ref
  1.5 0.0 copy-done
  1.5 251.1 %shard_map.73 = bf16[512,2048]{1,0:T(8,128)(2,1)} custom-call(s32[128]{0:T(128)} %select_reduce_fusion.wanted_ref, s32[96]{0:T(128)} %copy-done, s32[1,128]{1,0:T(1,128)} %bitcast.5, bf16[512,1024]{1,0:T(8,128)(2,1)} %q_ref.1, bf16[512,1024]{1,0:T(8,128)(2,1)} %k_ref.1, bf16[512,1024]{1,0:T(8,128)(2,1)} %v_ref.1, bf16[512,1024]{1,0:T(8,128)(2,1)} %pk_ref.1, ...), custom_call_target="tpu_custom_call" | custom-call | tf_op jit(solution)/shard_map/pallas_call | solution.py:486
  252.6 3.2 %copy.12 = bf16[512,2048]{1,0:T(8,128)(2,1)} copy(bf16[512,2048]{1,0:T(8,128)(2,1)} %shard_map.73) | data formatting | bytes 4194304
  (1 shorter events, 0.0 us)
Async XLA Ops:
  0.9 0.6 copy-start

commit v6 on v4

--- a/solution.py
+++ b/solution.py
@@ -283,8 +283,6 @@
     for c in z_copies:
         c.start()
     lax.fori_loop(17, 49, send_query, 0)
-    w_hop_wait(1)
-    w_hop(2)
     for d in range(1, NZ):
         table_copy(2 + d, NY, place(x, (z - d + NZ) % NZ, 0), me).wait_recv()
     x_copies = [
@@ -310,18 +308,12 @@
             )
             own_o[t * HEADS + h] = out
             own_l[t * HEADS + h] = lse
-        if t == 1:
-            w_hop_wait(2)
-            w_hop(3)
-        elif t == 2:
-            w_hop_wait(3)
-            w_hop(4)
     for h in range(HEADS):
         columns = slice(h * D_HEAD, (h + 1) * D_HEAD)
         vt[h] = pv_ref[:, columns].T
         kh[h] = pk_ref[:, columns]
-    w_hop_wait(4)
-    w_first(0)
+    w_hop_wait(1)
+    w_hop(2)
 
     for d in range(1, NX):
         table_copy(9 + d, NZ * NY, place((x - d + NX) % NX, 0, 0), me).wait_recv()
@@ -357,24 +349,38 @@
     recv_o[me] = out.astype(jnp.bfloat16)
     recv_l[me] = lse
 
-    def serve(step, carry):
-        source = moved(me, step, -sign)
-        q_copy(me, source).wait_recv()
-        out, lse = answer(source, recv_q[source])
-        recv_q[source] = out.astype(jnp.bfloat16)
-        send_l[source] = lse
-        o_copy(source, me).start()
-        l_copy(source, me).start()
-        return carry
-
-    lax.fori_loop(1, 9, serve, 0)
+    def serve(sources):
+        for source in sources:
+            q_copy(me, source).wait_recv()
+        found = [answer(source, recv_q[source]) for source in sources]
+        for source, (out, lse) in zip(sources, found):
+            recv_q[source] = out.astype(jnp.bfloat16)
+            send_l[source] = lse
+            o_copy(source, me).start()
+            l_copy(source, me).start()
+
+    def serve_three(turn, carry):
+        serve([moved(me, 2 + 3 * turn + j, -sign) for j in range(3)])
+        return carry
+
+    serve([moved(me, 1, -sign)])
+    lax.fori_loop(0, 3, serve_three, 0)
+    w_hop_wait(2)
+    w_hop(3)
+    lax.fori_loop(3, 6, serve_three, 0)
+    w_hop_wait(3)
+    w_hop(4)
+    lax.fori_loop(6, 10, serve_three, 0)
+    w_hop_wait(4)
+    w_first(0)
+    lax.fori_loop(10, 14, serve_three, 0)
     w_forward(0)
-    lax.fori_loop(9, 17, serve, 0)
+    lax.fori_loop(14, 18, serve_three, 0)
     w_settle(0)
     w_first(1)
-    lax.fori_loop(17, 80, serve, 0)
+    lax.fori_loop(18, 34, serve_three, 0)
     w_forward(1)
-    lax.fori_loop(80, PEERS, serve, 0)
+    lax.fori_loop(34, (PEERS - 2) // 3, serve_three, 0)
 
     w_settle(1)
 

time: 242 us -> 257 us (1.062)
  Pallas kernels: 237 us -> 252 us
    pallas_call x1, Pallas kernels: 237 us -> 252 us  [layer(): pl.pallas_call(layer_kernel, out_shape=jax.ShapeDtypeStruct((BLOCK, 2 * W...]
where the time goes in v6:
time: 257 us
  Pallas kernels  252 us (98%)
  local copies, waits for them, and re-layouts  4.05 us (2%)
    pallas_call x1, Pallas kernels, layer(): pl.pallas_call(layer_kernel, out_shape=jax.ShapeDtypeStruct((BLOCK, 2 * W...  252 us

profile of v6, /device:TPU:1, one launch (start us, length us, event | category | flops | bytes accessed | tf_op | source)
XLA Modules:
  0.0 257.2 jit_solution(2879301846815686335)
XLA Ops:
  0.0 0.8 copy.10
  0.8 0.1 eq.15.picked_ref
  0.9 0.0 copy-start
  0.9 0.6 select_reduce_fusion.wanted_ref
  1.5 0.0 copy-done
  1.5 252.5 %shard_map.73 = bf16[512,2048]{1,0:T(8,128)(2,1)} custom-call(s32[128]{0:T(128)} %select_reduce_fusion.wanted_ref, s32[96]{0:T(128)} %copy-done, s32[1,128]{1,0:T(1,128)} %bitcast.5, bf16[512,1024]{1,0:T(8,128)(2,1)} %q_ref.1, bf16[512,1024]{1,0:T(8,128)(2,1)} %k_ref.1, bf16[512,1024]{1,0:T(8,128)(2,1)} %v_ref.1, bf16[512,1024]{1,0:T(8,128)(2,1)} %pk_ref.1, ...), custom_call_target="tpu_custom_call" | custom-call | tf_op jit(solution)/shard_map/pallas_call | solution.py:492
  254.0 3.2 %copy.12 = bf16[512,2048]{1,0:T(8,128)(2,1)} copy(bf16[512,2048]{1,0:T(8,128)(2,1)} %shard_map.73) | data formatting | bytes 4194304
  (1 shorter events, 0.0 us)
Async XLA Ops:
  0.9 0.6 copy-start

commit v7 on v2

--- a/solution.py
+++ b/solution.py
@@ -59,7 +59,7 @@
         (((1,), (0,)), ((), ())),
         preferred_element_type=jnp.float32,
     )
-    return out / total, top + jnp.log2(total)
+    return out * (1.0 / total), top + jnp.log2(total)
 
 
 def layer_kernel(
@@ -259,6 +259,11 @@
         return carry
 
     lax.fori_loop(1, 17, send_query, 0)
+    for p in range(2):
+        base = w_pos(p) - z
+        for d in range(1, NZ):
+            w_copy(p, d - 1, base + (z - d + NZ) % NZ, 1, me).wait_recv()
+    w_first(0)
     for d in range(1, NY):
         table_copy(d - 1, 1, place(x, z, (y - d + NY) % NY), me).wait_recv()
     z_copies = [
@@ -266,12 +271,8 @@
     ]
     for c in z_copies:
         c.start()
-    lax.fori_loop(17, 49, send_query, 0)
-    for p in range(2):
-        base = w_pos(p) - z
-        for d in range(1, NZ):
-            w_copy(p, d - 1, base + (z - d + NZ) % NZ, 1, me).wait_recv()
-    w_first(0)
+    lax.fori_loop(17, 33, send_query, 0)
+    w_forward(0)
     for d in range(1, NZ):
         table_copy(2 + d, NY, place(x, (z - d + NZ) % NZ, 0), me).wait_recv()
     x_copies = [
@@ -280,8 +281,10 @@
     ]
     for c in x_copies:
         c.start()
-    lax.fori_loop(49, PEERS, send_query, 0)
-    w_forward(0)
+    lax.fori_loop(33, 41, send_query, 0)
+    w_settle(0)
+    w_first(1)
+    lax.fori_loop(41, PEERS, send_query, 0)
 
     for t in range(TILES):
         depth = (t + 1) * TILE
@@ -302,8 +305,6 @@
         columns = slice(h * D_HEAD, (h + 1) * D_HEAD)
         vt[h] = pv_ref[:, columns].T
         kh[h] = pk_ref[:, columns]
-    w_settle(0)
-    w_first(1)
 
     for d in range(1, NX):
         table_copy(9 + d, NZ * NY, place((x - d + NX) % NX, 0, 0), me).wait_recv()

time: 242 us -> 242 us (level)
  no operation moved by 1% of the time
where the time goes in v7:
time: 242 us
  Pallas kernels  237 us (98%)
  local copies, waits for them, and re-layouts  4.05 us (2%)
    pallas_call x1, Pallas kernels, layer(): pl.pallas_call(layer_kernel, out_shape=jax.ShapeDtypeStruct((BLOCK, 2 * W...  237 us

profile of v7, /device:TPU:1, one launch (start us, length us, event | category | flops | bytes accessed | tf_op | source)
XLA Modules:
  0.0 242.0 jit_solution(14622731920276427788)
XLA Ops:
  0.0 0.8 copy.10
  0.8 0.1 eq.15.picked_ref
  0.9 0.0 copy-start
  0.9 0.6 select_reduce_fusion.wanted_ref
  1.5 0.0 copy-done
  1.5 237.3 %shard_map.73 = bf16[512,2048]{1,0:T(8,128)(2,1)} custom-call(s32[128]{0:T(128)} %select_reduce_fusion.wanted_ref, s32[96]{0:T(128)} %copy-done, s32[1,128]{1,0:T(1,128)} %bitcast.5, bf16[512,1024]{1,0:T(8,128)(2,1)} %q_ref.1, bf16[512,1024]{1,0:T(8,128)(2,1)} %k_ref.1, bf16[512,1024]{1,0:T(8,128)(2,1)} %v_ref.1, bf16[512,1024]{1,0:T(8,128)(2,1)} %pk_ref.1, ...), custom_call_target="tpu_custom_call" | custom-call | tf_op jit(solution)/shard_map/pallas_call | solution.py:464
  238.9 3.2 %copy.12 = bf16[512,2048]{1,0:T(8,128)(2,1)} copy(bf16[512,2048]{1,0:T(8,128)(2,1)} %shard_map.73) | data formatting | bytes 4194304
  (1 shorter events, 0.0 us)
Async XLA Ops:
  0.9 0.6 copy-start
